TPU v7x, 32 devices: a whole 2x2x4 slice. The times are simulated.
32 devices in a mesh: dp: 4 (over z), seq: 8 (over y, x, core).
Axes of the slice: x: 2, y: 2, z: 4, core: 2. Of those that a mesh axis runs over, the one named last changes fastest.
Arguments:
- inputs: bfloat16 [4, 6144, 768], P('dp', 'seq'), may hold values from -6 to 6
- lengths: int32 [4, 784], P('dp'), may hold values from 0 to 256, as said below
- w_query: bfloat16 [768, 768], replicated, may hold values from -0.21875 to 0.21875
- b_query: float32 [768], replicated, may hold values from -3 to 3
- w_key: bfloat16 [768, 768], replicated, may hold values from -0.21875 to 0.21875
- w_value: bfloat16 [768, 768], replicated, may hold values from -0.21875 to 0.21875
- b_value: float32 [768], replicated, may hold values from -3 to 3
- w_out: bfloat16 [768, 768], replicated, may hold values from -0.875 to 0.875
- b_out: float32 [768], replicated, may hold values from -3 to 3
- gain_one: float32 [768], replicated, may hold values from 0.5 to 1.5
- shift_one: float32 [768], replicated, may hold values from -1.2 to 1.2
- w_up: bfloat16 [768, 3072], replicated, may hold values from -0.21875 to 0.21875
- b_up: float32 [3072], replicated, may hold values from -3 to 3
- w_down: bfloat16 [3072, 768], replicated, may hold values from -0.109375 to 0.109375
- b_down: float32 [768], replicated, may hold values from -3 to 3
- gain_two: float32 [768], replicated, may hold values from 0.5 to 1.5
- shift_two: float32 [768], replicated, may hold values from -1.2 to 1.2
- d_output: bfloat16 [4, 6144, 768], P('dp', 'seq'), may hold values from -6 to 6
Outputs:
- output: bfloat16 [4, 6144, 768], P('dp', 'seq')
- d_inputs: float32 [4, 6144, 768], P('dp', 'seq')
- g_w_query: float32 [768, 768], replicated
- g_b_query: float32 [768], replicated
- g_w_key: float32 [768, 768], replicated
- g_w_value: float32 [768, 768], replicated
- g_b_value: float32 [768], replicated
- g_w_out: float32 [768, 768], replicated
- g_b_out: float32 [768], replicated
- g_gain_one: float32 [768], replicated
- g_shift_one: float32 [768], replicated
- g_w_up: float32 [768, 3072], replicated
- g_b_up: float32 [3072], replicated
- g_w_down: float32 [3072, 768], replicated
- g_b_down: float32 [768], replicated
- g_gain_two: float32 [768], replicated
- g_shift_two: float32 [768], replicated
Inputs may be any that keep to these rules, and one draw needn't show every extreme that they name: `lengths`: every item has at most 256 tokens and each row has one of exactly 256; a zero length is an empty slot; each row ends with some padding.
All inputs are finite; a program needn't handle non-finite values.
Results may differ from a plain program's by a relative error of at most 0.014.
Values may be sent and summed in bfloat16 or wider, within the bound.
No kernel may reach another device: no remote copies, remote signals or barrier semaphores. Data moves between devices by JAX's collectives and lax.ppermute only.
A program may use at most 192 MiB of HBM per device.

v0:
```python
import jax
import jax.numpy as jnp
from jax import lax
from jax.sharding import PartitionSpec as P

HEADS = 12
HEAD_DIM = 64
ITEM_MOST = 256


scale_head = 0.125
masked_fill = -1e30


def extended(block, sides, width):
    for axis, dim in sides:
        count = lax.axis_size(axis)
        forward = [(i, i + 1) for i in range(count - 1)]
        backward = [(target, source) for source, target in forward]
        low = lax.ppermute(
            lax.slice_in_dim(block, block.shape[dim] - width, None, axis=dim), axis, forward
        )
        high = lax.ppermute(lax.slice_in_dim(block, 0, width, axis=dim), axis, backward)
        block = jnp.concatenate([low, block, high], axis=dim)
    return block


def passed_along(value, axis, steps):
    count = lax.axis_size(axis)
    initial, last = (max(0, -steps), min(count, count - steps))
    return lax.ppermute(value, axis, [(source, source + steps) for source in range(initial, last)])


def block_size(count):
    return max((d for d in range(1, min(count, 512) + 1) if count % d == 0))


def segment_ids(ends, positions):
    return jnp.searchsorted(ends, positions, side="right")


def project(left, right):
    return jnp.dot(left, right, preferred_element_type=jnp.float32)


def split_heads(matrix):
    return matrix.reshape(matrix.shape[0], HEADS, HEAD_DIM)


def norm_apply(hidden, gain, shift):
    mean = jnp.mean(hidden, axis=-1, keepdims=True)
    centered = hidden - mean
    rstd = lax.rsqrt(jnp.mean(centered * centered, axis=-1, keepdims=True) + 1e-12)
    return centered * rstd * gain + shift


def gelu_exact(values):
    return jax.nn.gelu(values, approximate=False)


def block_scores(query_h, key_h, query_seg, key_seg):
    scores = (
        jnp.einsum("qhd,khd->hqk", query_h, key_h, preferred_element_type=jnp.float32) * scale_head
    )
    allowed = (query_seg[:, None] == key_seg[None, :])[None]
    return (jnp.where(allowed, scores, masked_fill), allowed)


def pair_terms(query_h, dattn_h, lse, delta, query_seg, key_h, value_h, key_seg):
    scores, allowed = block_scores(query_h, key_h, query_seg, key_seg)
    probs = jnp.where(allowed, jnp.exp(scores - lse[:, :, None]), 0.0)
    dprob = jnp.einsum("qhd,khd->hqk", dattn_h, value_h, preferred_element_type=jnp.float32)
    dscore = (probs * (dprob - delta[:, :, None])).astype(jnp.bfloat16)
    return (probs.astype(jnp.bfloat16), dscore)


def body(
    inputs,
    lengths,
    w_query,
    b_query,
    w_key,
    w_value,
    b_value,
    w_out,
    b_out,
    gain_one,
    shift_one,
    w_up,
    b_up,
    w_down,
    b_down,
    gain_two,
    shift_two,
    d_output,
):
    rows, tok_local, width = inputs.shape
    reach = ITEM_MOST
    seq_size = lax.axis_size("seq")
    here = lax.axis_index("seq")
    row_len = seq_size * tok_local
    blk = block_size(tok_local)
    count_b = tok_local // blk
    local_pos = jnp.arange(tok_local, dtype=jnp.int32)
    positions = here * tok_local + local_pos
    ext_pos = here * tok_local - reach + jnp.arange(tok_local + 2 * reach, dtype=jnp.int32)
    inside = (ext_pos >= 0) & (ext_pos < row_len)
    flat = inputs.reshape(rows * tok_local, width)
    query_all = (project(flat, w_query) + b_query).astype(jnp.bfloat16)
    w_pair = jnp.concatenate([w_key, w_value], axis=1)
    b_pair = jnp.concatenate([jnp.zeros_like(b_value), b_value])
    pair_all = (project(flat, w_pair) + b_pair).astype(jnp.bfloat16)
    pair_ext = extended(pair_all.reshape(rows, tok_local, 2 * width), (("seq", 1),), reach)
    seg_list, ext_seg_list, valid_list, attn_list, lse_list = ([], [], [], [], [])
    row = 0
    ends = jnp.cumsum(lengths[row])
    query_seg = segment_ids(ends, positions)
    ext_seg = jnp.where(inside, segment_ids(ends, ext_pos), -1)
    query_h = split_heads(query_all)
    key_h = split_heads(pair_ext[row][:, :width])
    value_h = split_heads(pair_ext[row][:, width:])

    def forward_block(args):
        query_blk, seg_blk = args
        scores, allowed = block_scores(query_blk, key_h, seg_blk, ext_seg)
        top = jnp.max(scores, axis=-1, keepdims=True)
        weights = jnp.exp(scores - top)
        total = jnp.sum(weights, axis=-1, keepdims=True)
        probs = (weights / total).astype(jnp.bfloat16)
        attn = jnp.einsum("hqk,khd->qhd", probs, value_h, preferred_element_type=jnp.float32)
        return (attn, top[:, :, 0] + jnp.log(total[:, :, 0]))

    attn_b, lse_b = lax.map(
        forward_block,
        (query_h.reshape(count_b, blk, HEADS, HEAD_DIM), query_seg.reshape(count_b, blk)),
    )
    seg_list.append(query_seg)
    ext_seg_list.append(ext_seg)
    valid_list.append((positions < ends[-1]).astype(jnp.float32))
    attn_list.append(attn_b.reshape(tok_local, HEADS, HEAD_DIM))
    lse_list.append(lse_b)
    attn_exact = jnp.concatenate([a.reshape(tok_local, width) for a in attn_list], axis=0)
    attn_low = attn_exact.astype(jnp.bfloat16)
    valid_all = valid_list[0]
    resid_one = flat.astype(jnp.float32) + project(attn_low, w_out) + b_out
    mid, norm_back_one = jax.vjp(norm_apply, resid_one, gain_one, shift_one)
    mid_low = mid.astype(jnp.bfloat16)
    up = project(mid_low, w_up) + b_up
    act, gelu_back = jax.vjp(gelu_exact, up)
    act_low = act.astype(jnp.bfloat16)
    resid_two = mid + project(act_low, w_down) + b_down
    normed, norm_back_two = jax.vjp(norm_apply, resid_two, gain_two, shift_two)
    output = (normed * valid_all[:, None]).astype(jnp.bfloat16).reshape(rows, tok_local, width)
    d_result = d_output.reshape(rows * tok_local, width).astype(jnp.float32) * valid_all[:, None]
    d_resid_two, g_gain_two, g_shift_two = norm_back_two(d_result)
    d_down = d_resid_two.astype(jnp.bfloat16)
    g_b_down = jnp.sum(d_down, axis=0, dtype=jnp.float32)
    g_w_down = jnp.einsum("tf,td->fd", act_low, d_down, preferred_element_type=jnp.float32)
    d_act = jnp.einsum("td,fd->tf", d_down, w_down, preferred_element_type=jnp.float32)
    d_up = gelu_back(d_act)[0].astype(jnp.bfloat16)
    g_b_up = jnp.sum(d_up, axis=0, dtype=jnp.float32)
    g_w_up = jnp.einsum("td,tf->df", mid_low, d_up, preferred_element_type=jnp.float32)
    d_mid = d_resid_two + jnp.einsum("tf,df->td", d_up, w_up, preferred_element_type=jnp.float32)
    d_resid_one, g_gain_one, g_shift_one = norm_back_one(d_mid)
    d_branch = d_resid_one.astype(jnp.bfloat16)
    g_b_out = jnp.sum(d_branch, axis=0, dtype=jnp.float32)
    g_w_out = jnp.einsum("te,td->ed", attn_low, d_branch, preferred_element_type=jnp.float32)
    d_attn_all = jnp.einsum(
        "td,ed->te", d_branch, w_out, preferred_element_type=jnp.float32
    ).astype(jnp.bfloat16)
    row = 0
    dattn_h = split_heads(d_attn_all)
    delta_list = [jnp.sum(dattn_h.astype(jnp.float32) * attn_list[row], axis=-1)]
    dq_list, dk_list, dv_list = ([], [], [])
    row = 0
    query_h = split_heads(query_all)
    dattn_h = split_heads(d_attn_all)
    key_h = split_heads(pair_ext[row][:, :width])
    value_h = split_heads(pair_ext[row][:, width:])
    ext_seg = ext_seg_list[row]
    delta_b = jnp.swapaxes(delta_list[row].reshape(count_b, blk, HEADS), 1, 2)
    zeros_ext = jnp.zeros((tok_local + 2 * reach, HEADS, HEAD_DIM), jnp.float32)

    def back_block(state, args):
        d_key, d_value = state
        query_blk, dattn_blk, seg_blk, lse_blk, delta_blk = args
        probs_low, dscore = pair_terms(
            query_blk, dattn_blk, lse_blk, delta_blk, seg_blk, key_h, value_h, ext_seg
        )
        d_query = jnp.einsum("hqk,khd->qhd", dscore, key_h, preferred_element_type=jnp.float32)
        d_key = d_key + jnp.einsum(
            "hqk,qhd->khd", dscore, query_blk, preferred_element_type=jnp.float32
        )
        d_value = d_value + jnp.einsum(
            "hqk,qhd->khd", probs_low, dattn_blk, preferred_element_type=jnp.float32
        )
        return ((d_key, d_value), d_query)

    blocks = (
        query_h.reshape(count_b, blk, HEADS, HEAD_DIM),
        dattn_h.reshape(count_b, blk, HEADS, HEAD_DIM),
        seg_list[row].reshape(count_b, blk),
        lse_list[row],
        delta_b,
    )
    (d_key_ext, d_value_ext), d_query_b = lax.scan(back_block, (zeros_ext, zeros_ext), blocks)
    dq_list.append((d_query_b.reshape(tok_local, width) * scale_head).astype(jnp.bfloat16))
    ext_list = [
        jnp.concatenate([d_key_ext.reshape(-1, width), d_value_ext.reshape(-1, width)], axis=1)
    ]
    ext_all = jnp.stack(ext_list, axis=0)
    from_above = passed_along(ext_all[:, :reach].astype(jnp.bfloat16), "seq", -1).astype(
        jnp.float32
    )
    from_below = passed_along(
        ext_all[:, reach + tok_local :].astype(jnp.bfloat16), "seq", 1
    ).astype(jnp.float32)
    middle = ext_all[:, reach : reach + tok_local]
    middle = middle.at[:, :reach].add(from_below)
    middle = middle.at[:, tok_local - reach :].add(from_above)
    d_key_all = (
        (middle[:, :, :width] * scale_head).astype(jnp.bfloat16).reshape(rows * tok_local, width)
    )
    d_value_all = middle[:, :, width:].astype(jnp.bfloat16).reshape(rows * tok_local, width)
    d_query_all = dq_list[0]
    d_pair_all = jnp.concatenate([d_key_all, d_value_all], axis=1)
    g_w_query = jnp.einsum("td,te->de", flat, d_query_all, preferred_element_type=jnp.float32)
    g_pair = jnp.einsum("td,te->de", flat, d_pair_all, preferred_element_type=jnp.float32)
    g_w_key = g_pair[:, :width]
    g_w_value = g_pair[:, width:]
    g_b_query = jnp.sum(d_query_all, axis=0, dtype=jnp.float32)
    g_b_value = jnp.sum(d_value_all, axis=0, dtype=jnp.float32)
    d_inputs = d_resid_one + jnp.einsum(
        "te,de->td", d_query_all, w_query, preferred_element_type=jnp.float32
    )
    d_inputs = d_inputs + jnp.einsum(
        "te,de->td", d_pair_all, w_pair, preferred_element_type=jnp.float32
    )
    summed = lax.psum(
        (
            g_w_query,
            g_b_query,
            g_w_key,
            g_w_value,
            g_b_value,
            g_w_out,
            g_b_out,
            g_gain_one,
            g_shift_one,
            g_w_up,
            g_b_up,
            g_w_down,
            g_b_down,
            g_gain_two,
            g_shift_two,
        ),
        ("dp", "seq"),
    )
    return (
        output,
        d_inputs.reshape(rows, tok_local, width),
        summed[0],
        summed[1],
        summed[2],
        summed[3],
        summed[4],
        summed[5],
        summed[6],
        summed[7],
        summed[8],
        summed[9],
        summed[10],
        summed[11],
        summed[12],
        summed[13],
        summed[14],
    )


def solution(mesh):
    return jax.shard_map(
        body,
        mesh=mesh,
        in_specs=(
            P("dp", "seq", None),
            P("dp", None),
            P(),
            P(),
            P(),
            P(),
            P(),
            P(),
            P(),
            P(),
            P(),
            P(),
            P(),
            P(),
            P(),
            P(),
            P(),
            P("dp", "seq", None),
        ),
        out_specs=(
            P("dp", "seq", None),
            P("dp", "seq", None),
            P(),
            P(),
            P(),
            P(),
            P(),
            P(),
            P(),
            P(),
            P(),
            P(),
            P(),
            P(),
            P(),
            P(),
            P(),
        ),
        check_vma=False,
    )
```

profile of v0, /device:TPU:0, one launch (start us, length us, event | category | flops | bytes accessed | tf_op | source)
XLA Modules:
  0.0 1058.4 jit_solution(14197258861452672483)
XLA Ops:
  22.9 111.0 %while.79 = (s32[]{:T(128)}, u32[1280]{0:T(1024)}, u32[1280]{0:T(1024)S(1)}, s32[784]{0:T(1024)S(1)}, s32[]{:T(128)}, /*index=5*/s32[]{:T(128)}, s32[]{:T(128)}, s32[]{}) while((s32[]{:T(128)}, u32[1280]{0:T(1024)}, u32[1280]{0:T(1024)S(1)}, s32[784]{0:T(1024)S(1)}, s32[]{:T(128)}, /*index=5*/s32[]{:T(128)}, s32[]{:T(128)}, ...), condition=%wide.region_5.6_spmd.clone, body=%wide.region_4.5_spmd.clone.sunk | while | flops 26372 | bytes 92785 | solution.py:39
  133.9 81.7 %while.78 = (s32[]{:T(128)}, u32[768]{0:T(1024)}, u32[768]{0:T(1024)S(1)}, s32[784]{0:T(1024)S(1)}, s32[]{:T(128)}, /*index=5*/s32[]{:T(128)}, s32[]{:T(128)}, s32[]{}) while((s32[]{:T(128)}, u32[768]{0:T(1024)}, u32[768]{0:T(1024)S(1)}, s32[784]{0:T(1024)S(1)}, s32[]{:T(128)}, /*index=5*/s32[]{:T(128)}, s32[]{:T(128)}, s32[]{}) %tuple.154), condition=%wide.region_3.4_spmd.clone, body=%wide.region_2.3_spmd.clone.sunk | while | flops 15620 | bytes 54897 | solution.py:39
  246.0 76.4 %while.77 = (s32[]{:T(128)}, f32[2,384,12,64]{1,3,2,0:T(8,128)}, f32[2,12,384]{2,1,0:T(8,128)}, s32[2,384]{1,0:T(2,128)S(1)}, s32[1280]{0:T(1024)S(1)}, /*index=...) while((s32[]{:T(128)}, f32[2,384,12,64]{1,3,2,0:T(8,128)}, ...), condition=%wide.region_9.10_spmd, body=%wide.region_6.9_spmd.sunk | while | flops 1581215232 | bytes 172981904 | solution.py:133
  246.8 13.7 %fusion.131 = (f32[12,384]{1,0:T(8,128)S(1)}, f32[12,384,1280]{2,1,0:T(8,128)}) fusion(pred[384,1280]{1,0:T(8,128)(4,1)S(1)} %broadcast_compare_fusion.4, bf16[1280,12,64]{0,2,1:T(8,128)(2,1)} %get-tuple-element.865, bf16[2,384,12,64]{1,3,2,0:T(8,128)(2,1)} %get-tuple-element.864, s32[]{:T(128)S(6)} %copy.132), kind=kOutput, calls=%fused_computation.17.clone.1 | convolution fusion | flops 772664832 | bytes 26658820 | tf_op jit(solution)/shard_map/while/body/eval_jaxpr/qhd,khd->hqk/dot_general | solution.py:63
  260.5 11.5 %fusion.132 = f32[12,384]{1,0:T(8,128)S(1)} fusion(f32[12,384,1280]{2,1,0:T(8,128)} %get-tuple-element.765, f32[12,384]{1,0:T(8,128)S(1)} %get-tuple-element.766, pred[384,1280]{1,0:T(8,128)(4,1)S(1)} %broadcast_compare_fusion.4), kind=kLoop, calls=%fused_computation.18.clone.1 | loop fusion | flops 23588352 | bytes 24121344 | tf_op jit(solution)/shard_map/while/body/eval_jaxpr/reduce_sum | solution.py:128
  284.8 13.7 %fusion.131 = (f32[12,384]{1,0:T(8,128)S(1)}, f32[12,384,1280]{2,1,0:T(8,128)}) fusion(pred[384,1280]{1,0:T(8,128)(4,1)S(1)} %broadcast_compare_fusion.4, bf16[1280,12,64]{0,2,1:T(8,128)(2,1)} %get-tuple-element.865, bf16[2,384,12,64]{1,3,2,0:T(8,128)(2,1)} %get-tuple-element.864, s32[]{:T(128)S(6)} %copy.132), kind=kOutput, calls=%fused_computation.17.clone.1 | convolution fusion | flops 772664832 | bytes 26658820 | tf_op jit(solution)/shard_map/while/body/eval_jaxpr/qhd,khd->hqk/dot_general | solution.py:63
  298.5 11.5 %fusion.132 = f32[12,384]{1,0:T(8,128)S(1)} fusion(f32[12,384,1280]{2,1,0:T(8,128)} %get-tuple-element.765, f32[12,384]{1,0:T(8,128)S(1)} %get-tuple-element.766, pred[384,1280]{1,0:T(8,128)(4,1)S(1)} %broadcast_compare_fusion.4), kind=kLoop, calls=%fused_computation.18.clone.1 | loop fusion | flops 23588352 | bytes 24121344 | tf_op jit(solution)/shard_map/while/body/eval_jaxpr/reduce_sum | solution.py:128
  313.0 8.8 fusion.133
  329.4 28.5 %multiply_convert_fusion.1 = (bf16[768,3072]{1,0:T(8,128)(2,1)S(1)}, f32[768,3072]{1,0:T(8,128)}, f32[768,3072]{1,0:T(8,128)}) fusion(f32[3072]{0:T(1024)S(1)} %copy-done.49, bf16[768,3072]{1,0:T(8,128)(2,1)S(1)} %bitcast.196, f32[768,768]{0,1:T(8,128)S(1)} %get-tuple-element.592, f32[768]{0:T(1024)S(1)} %copy-done.53, f32[768]{0:T(1024)S(1)} %copy-done.45, ...), kind=kOutput, calls=%fused_computation.60 | convolution fusion | flops 3782541312 | bytes 30695424 | tf_op jit(solution)/shard_map/dot_general | solution.py:43
  368.4 13.7 %convert_reduce_fusion = (f32[3072]{0:T(1024)}, bf16[768,3072]{1,0:T(8,128)(2,1)}) fusion(f32[768,3072]{1,0:T(8,128)} %get-tuple-element.577, f32[768,3072]{1,0:T(8,128)} %get-tuple-element.593, f32[3072]{0:T(1024)S(1)} %copy-done.49, bf16[768,768]{0,1:T(8,128)(2,1)S(1)} %get-tuple-element.565, bf16[3072,768]{1,0:T(8,128)(2,1)S(1)} %bitcast.194), kind=kOutput, calls=%fused_computation.58 | convolution fusion | flops 3663983616 | bytes 29515776 | tf_op jit(solution)/shard_map/td,fd->tf/dot_general | solution.py:159
  408.4 9.0 fusion.67
  419.1 122.3 %while.80 = (s32[]{:T(128)}, f32[1280,12,64]{0,2,1:T(8,128)}, f32[1280,12,64]{0,2,1:T(8,128)}, f32[2,384,12,64]{1,3,2,0:T(8,128)}, bf16[2,384,12,64]{1,3,2,0:T(8...) while((s32[]{:T(128)}, f32[1280,12,64]{0,2,1:T(8,128)}, ...), condition=%wide.region_20.21_spmd.clone, body=%wide.region_19.20_spmd.clone.sunk | while | flops 3826483200 | bytes 163931888 | solution.py:206
  421.0 12.9 %exponential_select_fusion.2 = f32[12,384,1280]{2,1,0:T(8,128)} fusion(bf16[1280,12,64]{0,2,1:T(8,128)(2,1)} %get-tuple-element.903, f32[12,384]{1,0:T(8,128)S(1)} %dynamic-slice_bitcast_fusion.2, pred[384,1280]{1,0:T(8,128)(4,1)S(1)} %broadcast_compare_fusion.5, bf16[2,384,12,64]{1,3,2,0:T(8,128)(2,1)} %get-tuple-element.900, s32[]{:T(128)S(6)} %copy.142), kind=kOutput, calls=%fused_computation.32.clone.1 | convolution fusion | flops 778567680 | bytes 26658820 | tf_op jit(solution)/shard_map/while/body/eval_jaxpr/qhd,khd->hqk/dot_general | solution.py:63
  434.0 12.1 %bitcast_add_fusion.5 = f32[1280,12,64]{0,2,1:T(8,128)} fusion(f32[1280,12,64]{0,2,1:T(8,128)} %get-tuple-element.884, f32[12,384,1280]{2,1,0:T(8,128)} %exponential_select_fusion.2, pred[]{:T(512)S(6)} %compare.24, bf16[2,384,12,64]{1,3,2,0:T(8,128)(2,1)} %get-tuple-element.905, s32[]{:T(128)S(6)} %copy.142), kind=kOutput, calls=%fused_computation.35.clone.1 | convolution fusion | flops 762839040 | bytes 32047108 | tf_op jit(solution)/shard_map/while/body/eval_jaxpr/hqk,qhd->khd/dot_general | solution.py:194
  446.1 14.9 %multiply_convert_fusion.6 = bf16[12,384,1280]{2,1,0:T(8,128)(2,1)} fusion(f32[12,384,1280]{2,1,0:T(8,128)} %exponential_select_fusion.2, bf16[1280,12,64]{0,2,1:T(8,128)(2,1)} %get-tuple-element.906, f32[12,384]{1,0:T(8,128)S(1)} %bitcast.190, bf16[2,384,12,64]{1,3,2,0:T(8,128)(2,1)} %get-tuple-element.905, s32[]{:T(128)S(6)} %copy.142), kind=kOutput, calls=%fused_computation.31.clone.1 | convolution fusion | flops 772669440 | bytes 37963780 | tf_op jit(solution)/shard_map/while/body/eval_jaxpr/qhd,khd->hqk/dot_general | solution.py:72
  461.0 9.7 fusion.144
  481.6 12.9 %exponential_select_fusion.2 = f32[12,384,1280]{2,1,0:T(8,128)} fusion(bf16[1280,12,64]{0,2,1:T(8,128)(2,1)} %get-tuple-element.903, f32[12,384]{1,0:T(8,128)S(1)} %dynamic-slice_bitcast_fusion.2, pred[384,1280]{1,0:T(8,128)(4,1)S(1)} %broadcast_compare_fusion.5, bf16[2,384,12,64]{1,3,2,0:T(8,128)(2,1)} %get-tuple-element.900, s32[]{:T(128)S(6)} %copy.142), kind=kOutput, calls=%fused_computation.32.clone.1 | convolution fusion | flops 778567680 | bytes 26658820 | tf_op jit(solution)/shard_map/while/body/eval_jaxpr/qhd,khd->hqk/dot_general | solution.py:63
  494.5 13.2 %bitcast_add_fusion.5 = f32[1280,12,64]{0,2,1:T(8,128)} fusion(f32[1280,12,64]{0,2,1:T(8,128)} %get-tuple-element.884, f32[12,384,1280]{2,1,0:T(8,128)} %exponential_select_fusion.2, pred[]{:T(512)S(6)} %compare.24, bf16[2,384,12,64]{1,3,2,0:T(8,128)(2,1)} %get-tuple-element.905, s32[]{:T(128)S(6)} %copy.142), kind=kOutput, calls=%fused_computation.35.clone.1 | convolution fusion | flops 762839040 | bytes 32047108 | tf_op jit(solution)/shard_map/while/body/eval_jaxpr/hqk,qhd->khd/dot_general | solution.py:194
  507.7 14.9 %multiply_convert_fusion.6 = bf16[12,384,1280]{2,1,0:T(8,128)(2,1)} fusion(f32[12,384,1280]{2,1,0:T(8,128)} %exponential_select_fusion.2, bf16[1280,12,64]{0,2,1:T(8,128)(2,1)} %get-tuple-element.906, f32[12,384]{1,0:T(8,128)S(1)} %bitcast.190, bf16[2,384,12,64]{1,3,2,0:T(8,128)(2,1)} %get-tuple-element.905, s32[]{:T(128)S(6)} %copy.142), kind=kOutput, calls=%fused_computation.31.clone.1 | convolution fusion | flops 772669440 | bytes 37963780 | tf_op jit(solution)/shard_map/while/body/eval_jaxpr/qhd,khd->hqk/dot_general | solution.py:72
  522.6 9.7 fusion.144
  548.5 13.2 %fusion.83 = f32[3072,768]{1,0:T(8,128)} fusion(bf16[768,3072]{1,0:T(8,128)(2,1)} %copy-done.55, bf16[768,768]{0,1:T(8,128)(2,1)} %copy-done.30), kind=kOutput, calls=%fused_computation.164 | convolution fusion | flops 3623878656 | bytes 15335424 | tf_op jit(solution)/shard_map/tf,td->fd/dot_general | solution.py:158
  593.3 52.4 %all-reduce.2 = (f32[768]{0:T(1024)}, f32[768]{0:T(1024)}, f32[768]{0:T(1024)}, f32[768]{0:T(1024)}, f32[768]{0:T(1024)}, /*index=5*/f32[3072]{0:T(1024)}, f32[768]{0:T(1024)}, f32[768]{0:T(1024)}, f32[768]{0:T(1024)}) all-reduce(f32[768]{0:T(1024)} %reduce_sum.189, ...), channel_id=1, replica_groups=mesh['dp'=4,'seq'=8] {'dp','seq'}, use_global_device_ids=true, to_apply=%region_23.24 | all-reduce | flops 9216 | bytes 73728 | tf_op jit(solution)/shard_map/psum | solution.py:239
  645.7 382.7 %all-reduce.6.cloned.1.call-done = (f32[768,768]{0,1:T(8,128)}, f32[768,768]{0,1:T(8,128)}, f32[768,768]{0,1:T(8,128)}, f32[768,768]{1,0:T(8,128)}, f32[768,3072]{1,0:T(8,128)}, /*index=5*/f32[3072,768]{1,0:T(8,128)}) async-done(((f32[768,768]{0,1:T(8,128)}, f32[768,768]{0,1:T(8,128)}, f32[768,768]{0,1:T(8,128)}, f32[768,768]{1,0:T(8,128)}, f32[768,3072]{1,0:T(8,128)}, /*index=5*/f32[3072,768]{1,0:T(8,128)}), ...) | async-done | bytes 28311568 | tf_op jit(solution)/shard_map/psum | solution.py:239
  1038.2 9.3 copy.160
  (370 shorter events, 374.0 us)
Async XLA Ops:
  7.2 318.5 %copy-start = (bf16[768,768]{1,0:T(8,128)(2,1)S(1)}, bf16[768,768]{1,0:T(8,128)(2,1)}, u32[]{:S(2)}) copy-start(bf16[768,768]{1,0:T(8,128)(2,1)} %param.37) | copy-start | bytes 3538948
  7.2 1021.2 %all-reduce.6.cloned.1.call-start = ((), (), s32[]{:S(2)}) async-start(), calls=%async_computation | async-start | bytes 56623104 | tf_op jit(solution)/shard_map/psum | solution.py:239
  12.5 222.5 %collective-permute-start = (bf16[1,256,1536]{2,1,0:T(8,128)(2,1)}, bf16[1,256,1536]{2,1,0:T(8,128)(2,1)}, u32[]{:S(2)}, u32[]{:S(2)}) collective-permute-start(bf16[1,256,1536]{2,1,0:T(8,128)(2,1)} %get-tuple-element.587), channel_id=1, source_target_pairs={{0,1},{1,2},{2,3},{3,4},{4,5},{5,6},{6,7},{8,9},{9,10},{10,11},{11... | collective-permute-start | bytes 2359304 | tf_op jit(solution)/shard_map/ppermute | solution.py:20
  15.8 219.3 %collective-permute-start.1 = (bf16[1,256,1536]{2,1,0:T(8,128)(2,1)}, bf16[1,256,1536]{2,1,0:T(8,128)(2,1)}, u32[]{:S(2)}, u32[]{:S(2)}) collective-permute-start(bf16[1,256,1536]{2,1,0:T(8,128)(2,1)} %get-tuple-element.588), channel_id=1, source_target_pairs={{1,0},{2,1},{3,2},{4,3},{5,4},{6,5},{7,6},{9,8},{10,9},{11,10},{12... | collective-permute-start | bytes 2359304 | tf_op jit(solution)/shard_map/ppermute | solution.py:23
  260.5 14.5 %copy-start.1 = (f32[12,384,1280]{2,1,0:T(8,128)S(1)}, f32[12,384,1280]{2,1,0:T(8,128)}, u32[]{:S(2)}) copy-start(f32[12,384,1280]{2,1,0:T(8,128)} %get-tuple-element.765) | copy-start | bytes 70778880 | tf_op jit(solution)/shard_map/while
  298.5 14.5 %copy-start.1 = (f32[12,384,1280]{2,1,0:T(8,128)S(1)}, f32[12,384,1280]{2,1,0:T(8,128)}, u32[]{:S(2)}) copy-start(f32[12,384,1280]{2,1,0:T(8,128)} %get-tuple-element.765) | copy-start | bytes 70778880 | tf_op jit(solution)/shard_map/while
  325.8 32.2 %slice-start.4 = ((s8[4718592]{0:T(1024)(128)(4,1)}), s8[4194304]{0:T(1024)(128)(4,1)S(1)}, s32[]{:S(2)}) async-start(s8[4718592]{0:T(1024)(128)(4,1)} %bitcast.193), calls=%async_computation.5 | async-start | bytes 8388608
  327.0 63.1 %copy-start.12 = (f32[768,768]{0,1:T(8,128)}, f32[768,768]{0,1:T(8,128)S(1)}, u32[]{:S(2)}) copy-start(f32[768,768]{0,1:T(8,128)S(1)} %get-tuple-element.592) | copy-start | bytes 7077892
  327.1 63.0 %copy-start.36 = (f32[768]{0:T(1024)}, f32[768]{0:T(1024)S(1)}, u32[]{:S(2)}) copy-start(f32[768]{0:T(1024)S(1)} %broadcast_multiply_fusion.1) | copy-start | bytes 9220
  329.4 60.7 %copy-start.40 = (f32[768]{0:T(1024)}, f32[768]{0:T(1024)S(1)}, u32[]{:S(2)}) copy-start(f32[768]{0:T(1024)S(1)} %fusion.63) | copy-start | bytes 9220
  329.4 28.5 %slice-start.5 = ((s8[4718592]{0:T(1024)(128)(4,1)}), s8[524288]{0:T(1024)(128)(4,1)S(1)}, s32[]{:S(2)}) async-start(s8[4718592]{0:T(1024)(128)(4,1)} %bitcast.193), calls=%async_computation.6 | async-start | bytes 1048576
  329.4 28.5 %copy-start.52 = (f32[768]{0:T(1024)S(1)}, f32[768]{0:T(1024)}, u32[]{:S(2)}) copy-start(f32[768]{0:T(1024)} %param.44) | copy-start | bytes 9220
  368.3 13.7 %copy-start.30 = (bf16[768,768]{0,1:T(8,128)(2,1)}, bf16[768,768]{0,1:T(8,128)(2,1)S(1)}, u32[]{:S(2)}) copy-start(bf16[768,768]{0,1:T(8,128)(2,1)S(1)} %get-tuple-element.565) | copy-start | bytes 3538948
  396.2 6.1 copy-start.9
  402.3 6.1 copy-start.13
  402.3 6.1 copy-start.37
  461.0 9.7 copy-start.2
  522.6 9.7 copy-start.2
  548.5 21.1 %copy-start.5 = (f32[1,1280,1536]{1,2,0:T(8,128)}, f32[1,1280,1536]{1,2,0:T(8,128)S(1)}, u32[]{:S(2)}) copy-start(f32[1,1280,1536]{1,2,0:T(8,128)S(1)} %maximum_bitcast_fusion) | copy-start | bytes 23592964
  561.8 13.3 %collective-permute-start.2 = (bf16[1,256,1536]{1,2,0:T(8,128)(2,1)S(1)}, bf16[1,256,1536]{1,2,0:T(8,128)(2,1)S(1)}, u32[]{:S(2)}, u32[]{:S(2)}) collective-permute-start(bf16[1,256,1536]{1,2,0:T(8,128)(2,1)S(1)} %get-tuple-element.583), channel_id=1, source_target_pairs={{0,1},{1,2},{2,3},{3,4},{4,5},{5,6},{6,7},{8,9},{9,10},{10,11},{11... | collective-permute-start | bytes 2359304 | tf_op jit(solution)/shard_map/ppermute | solution.py:31
  568.1 9.1 collective-permute-start.3
  1036.8 10.7 %slice-start.1 = ((s8[9437184]{0:T(1024)(128)(4,1)}), s8[4194304]{0:T(1024)(128)(4,1)S(1)}, s32[]{:S(2)}) async-start(s8[9437184]{0:T(1024)(128)(4,1)} %bitcast.184), calls=%async_computation.2 | async-start | bytes 8388608
  1038.2 9.3 slice-start.2
  1038.2 9.3 slice-start.3
  (48 other events, 151.7 us)
Sparse Core Ops, SparseCore 0:
  582.5 445.8 all-reduce.5
where the time goes:
time: 1070 us; the launch traced here: 1060 us
  waiting for transfers between devices  383 us (36%)
  matrix products  258 us (24%)
  local copies, waits for them, and re-layouts  221 us (21%)
  other arithmetic  118 us (11%)
  blocking collectives  52.4 us (5%)
  between operations  15.1 us (1%)
    psum x1, waiting for transfers between devices, body(): lax.psum((g_w_query, g_b_query, g_w_key, g_w_value, g_b_value, g_w_out, g...  383 us
    gather x20, local copies, waits for them, and re-layouts, segment_ids(): return jnp.searchsorted(ends, positions, side='right')  129 us
    dot_general x4, matrix products, block_scores(): jnp.einsum('qhd,khd->hqk', query_h, key_h, preferred_element_type=jnp.flo...  53.3 us
    psum x1, blocking collectives, body(): lax.psum((g_w_query, g_b_query, g_w_key, g_w_value, g_b_value, g_w_out, g...  52.4 us
    unnamed x134, local copies, waits for them, and re-layouts  41.7 us
    dot_general x5, matrix products, project(): return jnp.dot(left, right, preferred_element_type=jnp.float32)  40.2 us
    select_n x40, other arithmetic, segment_ids(): return jnp.searchsorted(ends, positions, side='right')  38.8 us
    dot_general x2, matrix products, pair_terms(): jnp.einsum('qhd,khd->hqk', dattn_h, value_h, preferred_element_type=jnp.f...  29.8 us
  transfers between devices with their start and end apart: 5, of which 1 were waited for; matrix products, arithmetic and copies ran while one was open for 22% of the time, Pallas kernels for 0%

commit v1 on v0

v1 whole, which is shorter than its diff:
```python
import functools

import jax
import jax.numpy as jnp
from jax import lax
from jax.experimental import pallas as pl
from jax.experimental.pallas import tpu as pltpu
from jax.sharding import PartitionSpec as P

HEADS = 12
HEAD_DIM = 64
ITEM_MOST = 256
EPS = 1e-12
SCALE = 0.125
MASKED = -1e30
FAR = 1e9
TILE = 128
PAIR = 2 * HEAD_DIM
WIDTHS = (256, 384, 640)
ROWS = 256
PARTS = 8
VMEM_MOST = 60 * 1024 * 1024

bf16 = jnp.bfloat16
f32 = jnp.float32
i32 = jnp.int32
ANY = pl.BlockSpec(memory_space=pl.ANY)
SMEM = pl.BlockSpec(memory_space=pltpu.SMEM)
VMEM = pl.BlockSpec(memory_space=pltpu.VMEM)


def params(**kw):
    return pltpu.CompilerParams(vmem_limit_bytes=VMEM_MOST, **kw)


def cost(flops, nbytes, trans=0):
    return pl.CostEstimate(flops=int(flops), bytes_accessed=int(nbytes), transcendentals=int(trans))


def mm(a, b):
    return lax.dot_general(a, b, (((1,), (0,)), ((), ())), preferred_element_type=f32)


def mm_nt(a, b):
    return lax.dot_general(a, b, (((1,), (1,)), ((), ())), preferred_element_type=f32)


def mm_tn(a, b):
    return lax.dot_general(a, b, (((0,), (0,)), ((), ())), preferred_element_type=f32)


def front_kernel(place, lengths, x, wq, wk, wv, bq, bv, q, k, v, se, spans, wbuf, sems):
    copies = [
        pltpu.make_async_copy(w, wbuf.at[i], sems.at[i]) for i, w in enumerate((wq, wk, wv))
    ]
    for c in copies:
        c.start()
    slots = lengths.shape[1]
    tokens = x.shape[0]
    ext = se.shape[1]
    reach = (ext - tokens) // 2
    step = max(d for d in range(8, 129, 8) if slots % d == 0)
    start = place[0] - reach
    pos = (lax.broadcasted_iota(i32, (1, ext), 1) + start).astype(f32)
    sizes = lengths[...].astype(f32)

    def scan(c, state):
        low, high = state
        index = lax.broadcasted_iota(i32, (step, slots), 0) + c * step
        upto = lax.broadcasted_iota(i32, (step, slots), 1) <= index
        ends = jnp.sum(jnp.where(upto, sizes, 0.0), axis=1, keepdims=True)
        before = ends <= pos
        low = jnp.maximum(low, jnp.max(jnp.where(before, ends, 0.0), axis=0, keepdims=True))
        high = jnp.minimum(high, jnp.min(jnp.where(before, FAR, ends), axis=0, keepdims=True))
        return low, high

    low, high = lax.fori_loop(
        0, slots // step, scan, (jnp.zeros((1, ext), f32), jnp.full((1, ext), FAR, f32))
    )
    real = (pos >= 0.0) & (high < FAR)
    local = lax.broadcasted_iota(i32, (1, ext), 1).astype(f32)
    offset = start.astype(f32)
    own = (local >= reach) & (local < reach + tokens)
    low_e = jnp.where(real, low - offset, local)
    high_e = jnp.where(real, high - offset, local + 1.0)
    shared = real & (
        ((local < reach) & (high_e > reach)) | ((local >= reach + tokens) & (low_e < reach + tokens))
    )
    used = own | shared
    low_e = jnp.where(used, low_e, 0.0)
    high_e = jnp.where(used, high_e, 0.0)
    se[0:1, :] = low_e
    se[1:2, :] = high_e
    spans[0] = jnp.sum(sizes).astype(i32)
    for t in range(ext // TILE):
        sl = slice(t * TILE, (t + 1) * TILE)
        some = high_e[:, sl] > low_e[:, sl]
        first = jnp.min(jnp.where(some, low_e[:, sl], FAR)).astype(i32)
        last = jnp.max(jnp.where(some, high_e[:, sl], -1.0)).astype(i32)
        at = first & ~15
        span = last - at
        kind = jnp.where(span <= WIDTHS[0], 1, jnp.where(span <= WIDTHS[1], 2, 3))
        wide = min(max(t * TILE - reach, 0), ext - WIDTHS[2])
        at = jnp.where(
            kind == 1,
            jnp.minimum(at, ext - WIDTHS[0]),
            jnp.where(kind == 2, jnp.minimum(at, ext - WIDTHS[1]), wide),
        )
        spans[8 + 2 * t] = jnp.where(last < 0, 0, kind)
        spans[9 + 2 * t] = at

    for i, (w, b, out) in enumerate(((wq, bq, q), (wk, None, k), (wv, bv, v))):
        copies[i].wait()

        def rows(r, _, i=i, b=b, out=out):
            at = pl.ds(pl.multiple_of(r * ROWS, ROWS), ROWS)
            y = mm(x[at, :], wbuf[i])
            if b is not None:
                y = y + b[...]
            y = y.astype(bf16)
            if out is q:
                y = y * bf16(SCALE)
            out[at, :] = y
            return 0

        lax.fori_loop(0, tokens // ROWS, rows, 0)


def front(place, lengths, x, wq, wk, wv, bq, bv, reach):
    tokens, width = x.shape
    ext = tokens + 2 * reach
    out = jax.ShapeDtypeStruct((tokens, width), bf16)
    return pl.pallas_call(
        front_kernel,
        out_shape=(
            out,
            out,
            out,
            jax.ShapeDtypeStruct((8, ext), f32),
            jax.ShapeDtypeStruct((8 + 2 * (ext // TILE),), i32),
        ),
        in_specs=[SMEM, VMEM, VMEM, ANY, ANY, ANY, VMEM, VMEM],
        out_specs=(VMEM, VMEM, VMEM, VMEM, SMEM),
        scratch_shapes=[pltpu.VMEM((3, width, width), bf16), pltpu.SemaphoreType.DMA((3,))],
        compiler_params=params(),
        cost_estimate=cost(6 * tokens * width * width, 8 * tokens * width),
        name="front",
    )(place, lengths, x, wq, wk, wv, bq, bv)


def tile_bias(se, t, at, width):
    base = pl.multiple_of(t * TILE, TILE)
    low = se[0:1, pl.ds(base, TILE)]
    high = se[1:2, pl.ds(base, TILE)]
    key = (lax.broadcasted_iota(i32, (width, TILE), 0) + at).astype(f32)
    one = jnp.where((key >= low) & (key < high), 0.0, MASKED)
    some = jnp.where(high > low, 1.0, 0.0)
    return jnp.concatenate([one, one], axis=1), jnp.concatenate([some, some], axis=1)


def stacked(pair):
    lane = lax.broadcasted_iota(i32, pair.shape, 1)
    zero = jnp.zeros_like(pair)
    return jnp.concatenate(
        [jnp.where(lane < HEAD_DIM, pair, zero), jnp.where(lane < HEAD_DIM, zero, pair)], axis=0
    )


def unstacked(both):
    own = jnp.concatenate([both[:HEAD_DIM, :TILE], both[HEAD_DIM:, TILE:]], axis=0)
    return own.T


def attend_kernel(spans, se, q, k, v, xl, xr, wk, wv, bv, attn, kh, vh, kx, vx, wbuf, sems):
    tokens, width = q.shape
    reach = xl.shape[0]
    copies = [
        pltpu.make_async_copy(wk, wbuf.at[0], sems.at[0]),
        pltpu.make_async_copy(wv, wbuf.at[1], sems.at[1]),
        pltpu.make_async_copy(k, kx.at[pl.ds(reach, tokens)], sems.at[2]),
        pltpu.make_async_copy(v, vx.at[pl.ds(reach, tokens)], sems.at[3]),
    ]
    for c in copies:
        c.start()
    copies[0].wait()
    for part, at in ((xl, 0), (xr, reach + tokens)):
        y = mm(part[...], wbuf[0]).astype(bf16)
        kx[at : at + reach, :] = y
        kh[(0 if at == 0 else reach) : (reach if at == 0 else 2 * reach), :] = y
    copies[1].wait()
    for part, at in ((xl, 0), (xr, reach + tokens)):
        y = (mm(part[...], wbuf[1]) + bv[...]).astype(bf16)
        vx[at : at + reach, :] = y
        vh[(0 if at == 0 else reach) : (reach if at == 0 else 2 * reach), :] = y
    copies[2].wait()
    copies[3].wait()

    def tile(t, at, span):
        bias, _ = tile_bias(se, t, at, span)
        rows = pl.ds(pl.multiple_of(t * TILE - reach, TILE), TILE)
        window = pl.ds(pl.multiple_of(at, 16), span)
        for p in range(width // PAIR):
            lanes = slice(p * PAIR, (p + 1) * PAIR)
            scores = mm_nt(kx[window, lanes], stacked(q[rows, lanes])) + bias
            top = jnp.max(scores, axis=0, keepdims=True)
            weights = jnp.exp(scores - top)
            total = jnp.sum(weights, axis=0, keepdims=True)
            both = mm_tn(vx[window, lanes], weights.astype(bf16)) / total
            attn[rows, lanes] = unstacked(both).astype(bf16)

    def each(t, _):
        kind, at = spans[8 + 2 * t], spans[9 + 2 * t]
        for i, span in enumerate(WIDTHS):
            pl.when(kind == i + 1)(functools.partial(tile, t, at, span))
        return 0

    lax.fori_loop(reach // TILE, (reach + tokens) // TILE, each, 0)


def attend(spans, se, q, k, v, xl, xr, wk, wv, bv):
    tokens, width = q.shape
    reach = xl.shape[0]
    ext = tokens + 2 * reach
    halo = jax.ShapeDtypeStruct((2 * reach, width), bf16)
    return pl.pallas_call(
        attend_kernel,
        out_shape=(jax.ShapeDtypeStruct((tokens, width), bf16), halo, halo),
        in_specs=[SMEM, VMEM, VMEM, ANY, ANY, VMEM, VMEM, ANY, ANY, VMEM],
        out_specs=(VMEM, VMEM, VMEM),
        scratch_shapes=[
            pltpu.VMEM((ext, width), bf16),
            pltpu.VMEM((ext, width), bf16),
            pltpu.VMEM((2, width, width), bf16),
            pltpu.SemaphoreType.DMA((4,)),
        ],
        compiler_params=params(),
        cost_estimate=cost(8e9, 12 * tokens * width),
        name="attend",
    )(spans, se, q, k, v, xl, xr, wk, wv, bv)


def attend_back_kernel(
    spans, se, q, k, v, do, kh, vh, xl, xr, dl, dr, wq, bq, dq, dk, dv, qx, kx, vx, dox, dkx, dvx, wbuf, sems
):
    tokens, width = q.shape
    reach = xl.shape[0]
    ext = kx.shape[0]
    own, low, high = pl.ds(reach, tokens), pl.ds(0, reach), pl.ds(reach + tokens, reach)
    pairs = [
        (wq, wbuf),
        (q, qx.at[own]),
        (k, kx.at[own]),
        (v, vx.at[own]),
        (do, dox.at[own]),
        (kh.at[pl.ds(0, reach)], kx.at[low]),
        (kh.at[pl.ds(reach, reach)], kx.at[high]),
        (vh.at[pl.ds(0, reach)], vx.at[low]),
        (vh.at[pl.ds(reach, reach)], vx.at[high]),
        (dl, dox.at[low]),
        (dr, dox.at[high]),
    ]
    copies = [pltpu.make_async_copy(a, b, sems.at[i]) for i, (a, b) in enumerate(pairs)]
    for c in copies:
        c.start()
    dkx[...] = jnp.zeros_like(dkx)
    dvx[...] = jnp.zeros_like(dvx)
    copies[0].wait()
    for part, at in ((xl, 0), (xr, reach + tokens)):
        y = (mm(part[...], wbuf[...]) + bq[...]).astype(bf16)
        qx[at : at + reach, :] = y * bf16(SCALE)
    for c in copies[1:]:
        c.wait()

    def tile(t, at, span):
        bias, some = tile_bias(se, t, at, span)
        rows = pl.ds(pl.multiple_of(t * TILE, TILE), TILE)
        window = pl.ds(pl.multiple_of(at, 16), span)
        inside = (t >= reach // TILE) & (t < (reach + tokens) // TILE)
        for p in range(width // PAIR):
            lanes = slice(p * PAIR, (p + 1) * PAIR)
            key, value = kx[window, lanes], vx[window, lanes]
            query, dout = stacked(qx[rows, lanes]), stacked(dox[rows, lanes])
            scores = mm_nt(key, query) + bias
            top = jnp.max(scores, axis=0, keepdims=True)
            weights = jnp.exp(scores - top)
            total = jnp.sum(weights, axis=0, keepdims=True)
            probs = weights * (some / total)
            dprob = mm_nt(value, dout)
            delta = jnp.sum(probs * dprob, axis=0, keepdims=True)
            dscore = (probs * (dprob - delta)).astype(bf16)
            dvx[window, lanes] += mm(probs.astype(bf16), dout)
            dkx[window, lanes] += mm(dscore, query)

            @pl.when(inside)
            def _(key=key, dscore=dscore, lanes=lanes):
                here = pl.ds(pl.multiple_of(t * TILE - reach, TILE), TILE)
                dq[here, lanes] = (unstacked(mm_tn(key, dscore)) * SCALE).astype(bf16)

    def each(t, _):
        kind, at = spans[8 + 2 * t], spans[9 + 2 * t]
        for i, span in enumerate(WIDTHS):
            pl.when(kind == i + 1)(functools.partial(tile, t, at, span))
        return 0

    lax.fori_loop(0, ext // TILE, each, 0)
    dk[...] = dkx[reach : reach + tokens, :].astype(bf16)
    dv[...] = dvx[reach : reach + tokens, :].astype(bf16)


def attend_back(spans, se, q, k, v, do, kh, vh, xl, xr, dl, dr, wq, bq):
    tokens, width = q.shape
    reach = xl.shape[0]
    ext = tokens + 2 * reach
    out = jax.ShapeDtypeStruct((tokens, width), bf16)
    return pl.pallas_call(
        attend_back_kernel,
        out_shape=(out, out, out),
        in_specs=[SMEM, VMEM] + [ANY] * 6 + [VMEM, VMEM] + [ANY] * 3 + [VMEM],
        out_specs=(VMEM, VMEM, VMEM),
        scratch_shapes=[pltpu.VMEM((ext, width), bf16)] * 4
        + [pltpu.VMEM((ext, width), f32)] * 2
        + [pltpu.VMEM((width, width), bf16), pltpu.SemaphoreType.DMA((11,))],
        compiler_params=params(),
        cost_estimate=cost(16e9, 20 * tokens * width),
        name="attend_back",
    )(spans, se, q, k, v, do, kh, vh, xl, xr, dl, dr, wq, bq)


def write_group(block, send, keep, buf, sems, place):
    here, layer = place[1], place[2]
    half = buf.shape[1] // 2
    layers = place_layers(half)
    chunk = half // layers

    def copies(slot, x, y, out):
        return (
            pltpu.make_async_copy(
                buf.at[slot, pl.ds(0, half)],
                out.at[pl.ds(pl.multiple_of((2 * x + y) * half, half), half)],
                sems.at[slot, 0],
            ),
            pltpu.make_async_copy(
                buf.at[slot, pl.ds(half, half)],
                out.at[pl.ds(pl.multiple_of((4 + 2 * y + x) * half, half), half)],
                sems.at[slot, 1],
            ),
        )

    for core, out in ((1, send), (0, keep)):

        def step(j, _, core=core, out=out):
            x, y = j & 1, j >> 1
            part = (core + 2 * x + 4 * y) ^ here
            slot = j & 1
            value = block(part).astype(bf16)

            def free():
                for c in copies(slot, x, y, out):
                    c.wait()

            if core == 1:
                pl.when(j >= 2)(free)
            else:
                free()
            for z in range(layers):
                to = (z ^ layer) * chunk
                buf[slot, pl.ds(pl.multiple_of(to, chunk), chunk), :] = value[z * chunk : (z + 1) * chunk]
                buf[slot, pl.ds(pl.multiple_of(half + to, chunk), chunk), :] = value[
                    half + z * chunk : half + (z + 1) * chunk
                ]
            for c in copies(slot, x, y, out):
                c.start()
            return 0

        lax.fori_loop(0, PARTS // 2, step, 0)
    for slot in range(2):
        for c in copies(slot, 0, 0, keep):
            c.wait()


LAYERS = [4]


def place_layers(half):
    return LAYERS[0]


def group_shapes(rows, width):
    return (jax.ShapeDtypeStruct((rows // 2, width), bf16),) * 2


def group_scratch(rows, width):
    return [pltpu.VMEM((2, rows // PARTS, width), bf16), pltpu.SemaphoreType.DMA((2, 2))]


def gelu_both(z):
    u = jnp.abs(z) * 0.7071067811865476
    t = 1.0 / (1.0 + 0.3275911 * u)
    bell = jnp.exp(-0.5 * z * z)
    poly = t * (
        0.5 * 0.254829592
        + t * (0.5 * -0.284496736 + t * (0.5 * 1.421413741 + t * (0.5 * -1.453152027 + t * (0.5 * 1.061405429))))
    )
    tail = poly * bell
    cdf = jnp.where(z >= 0.0, 1.0 - tail, tail)
    return z * cdf, cdf + z * bell * 0.3989422804014327


def center(v):
    mean = jnp.mean(v, axis=1, keepdims=True)
    c = v - mean
    rstd = lax.rsqrt(jnp.mean(c * c, axis=1, keepdims=True) + EPS)
    return c * rstd, rstd


def center_back(e, xhat, rstd):
    return rstd * (
        e - jnp.mean(e, axis=1, keepdims=True) - xhat * jnp.mean(e * xhat, axis=1, keepdims=True)
    )


def colsum(v):
    return jnp.sum(v, axis=0, keepdims=True)


def chain_kernel(
    place, spans, attn, x, dy, wo, wu, wd, bo, g1, s1, bu, bd, g2, s2,
    out, slope, mid_low, xhat1, rstd1, d_two, d_down, vec, send, keep,
    wo_b, wu_b, wd_b, act, dd, buf, wsems, gsems,
):
    i = pl.program_id(0)
    ff = wu.shape[1]
    width = x.shape[1]
    copies = [
        pltpu.make_async_copy(a, b, wsems.at[n]) for n, (a, b) in enumerate(((wo, wo_b), (wu, wu_b), (wd, wd_b)))
    ]

    @pl.when(i == 0)
    def _():
        for c in copies:
            c.start()
        vec[...] = jnp.zeros_like(vec)
        copies[0].wait()

    one = x[...].astype(f32) + mm(attn[...], wo_b[...]) + bo[...]
    xh1, r1 = center(one)
    mid = xh1 * g1[...] + s1[...]
    low = mid.astype(bf16)
    xhat1[...] = xh1
    rstd1[...] = jnp.broadcast_to(r1, rstd1.shape)
    mid_low[...] = low

    @pl.when(i == 0)
    def _():
        copies[1].wait()
        copies[2].wait()

    rows = pl.ds(pl.multiple_of(i * ROWS, ROWS), ROWS)
    two = mid + bd[...]
    step = 512
    for c in range(ff // step):
        cols = slice(c * step, (c + 1) * step)
        a, s = gelu_both(mm(low, wu_b[:, cols]) + bu[:, cols])
        a = a.astype(bf16)
        act[rows, cols] = a
        slope[:, cols] = s.astype(bf16)
        two = two + mm(a, wd_b[cols, :])
    xh2, r2 = center(two)
    token = place[0] + i * ROWS + lax.broadcasted_iota(i32, (ROWS, 1), 0)
    valid = jnp.where(token < spans[0], 1.0, 0.0)
    out[...] = ((xh2 * g2[...] + s2[...]) * valid).astype(bf16)
    d = dy[...].astype(f32) * valid
    vec[1:2, :] += colsum(d * xh2)
    vec[2:3, :] += colsum(d)
    d2 = center_back(d * g2[...], xh2, r2)
    d_two[...] = d2
    d2 = d2.astype(bf16)
    d_down[...] = d2
    dd[rows, :] = d2
    vec[0:1, :] += colsum(d2.astype(f32))

    @pl.when(i == pl.num_programs(0) - 1)
    def _():
        size = ff // PARTS

        def block(part):
            return mm_tn(act[:, pl.ds(pl.multiple_of(part * size, size), size)], dd[...])

        write_group(block, send, keep, buf, gsems, place)


def chain(place, spans, attn, x, dy, wo, wu, wd, bo, g1, s1, bu, bd, g2, s2):
    tokens, width = x.shape
    ff = wu.shape[1]
    tok = lambda n: pl.BlockSpec((ROWS, n), lambda i: (i, 0))
    row = lambda n: pl.BlockSpec((1, n), lambda i: (0, 0))
    shape = lambda n, t: jax.ShapeDtypeStruct((tokens, n), t)
    return pl.pallas_call(
        chain_kernel,
        grid=(tokens // ROWS,),
        out_shape=(
            shape(width, bf16),
            shape(ff, bf16),
            shape(width, bf16),
            shape(width, f32),
            shape(128, f32),
            shape(width, f32),
            shape(width, bf16),
            jax.ShapeDtypeStruct((8, width), f32),
        )
        + group_shapes(ff, width),
        in_specs=[SMEM, SMEM, tok(width), tok(width), tok(width), ANY, ANY, ANY]
        + [row(width), row(width), row(width), row(ff), row(width), row(width), row(width)],
        out_specs=(
            tok(width),
            tok(ff),
            tok(width),
            tok(width),
            tok(128),
            tok(width),
            tok(width),
            pl.BlockSpec((8, width), lambda i: (0, 0)),
            ANY,
            ANY,
        ),
        scratch_shapes=[
            pltpu.VMEM((width, width), bf16),
            pltpu.VMEM((width, ff), bf16),
            pltpu.VMEM((ff, width), bf16),
            pltpu.VMEM((tokens, ff), bf16),
            pltpu.VMEM((tokens, width), bf16),
        ]
        + group_scratch(ff, width)[:1]
        + [pltpu.SemaphoreType.DMA((3,))]
        + group_scratch(ff, width)[1:],
        compiler_params=params(dimension_semantics=("arbitrary",)),
        cost_estimate=cost(2 * tokens * width * (width + 3 * ff), 30 * tokens * width, 2 * tokens * ff),
        name="chain",
    )(place, spans, attn, x, dy, wo, wu, wd, bo, g1, s1, bu, bd, g2, s2)


def back_kernel(
    d_two, d_down, slope, xhat1, rstd1, wd, wu, wo, g1,
    d_up, d_one, d_branch, d_attn, vec, wd_b, wu_b, wo_b, wsems,
):
    i = pl.program_id(0)
    ff = wu.shape[1]
    width = d_two.shape[1]
    copies = [
        pltpu.make_async_copy(a, b, wsems.at[n]) for n, (a, b) in enumerate(((wd, wd_b), (wu, wu_b), (wo, wo_b)))
    ]

    @pl.when(i == 0)
    def _():
        for c in copies:
            c.start()
        vec[...] = jnp.zeros_like(vec)
        for c in copies:
            c.wait()

    d_mid = d_two[...]
    dd = d_down[...]
    step = width
    for c in range(ff // step):
        cols = slice(c * step, (c + 1) * step)
        du = (slope[:, cols].astype(f32) * mm_nt(dd, wd_b[cols, :])).astype(bf16)
        d_up[:, cols] = du
        vec[3 + c : 4 + c, :] += colsum(du.astype(f32))
        d_mid = d_mid + mm_nt(du, wu_b[:, cols])
    xh = xhat1[...]
    vec[0:1, :] += colsum(d_mid * xh)
    vec[1:2, :] += colsum(d_mid)
    d1 = center_back(d_mid * g1[...], xh, rstd1[:, 0:1])
    d_one[...] = d1
    d1 = d1.astype(bf16)
    d_branch[...] = d1
    vec[2:3, :] += colsum(d1.astype(f32))
    d_attn[...] = mm_nt(d1, wo_b[...]).astype(bf16)


def back(d_two, d_down, slope, xhat1, rstd1, wd, wu, wo, g1):
    tokens, width = d_two.shape
    ff = wu.shape[1]
    tok = lambda n: pl.BlockSpec((ROWS, n), lambda i: (i, 0))
    shape = lambda n, t: jax.ShapeDtypeStruct((tokens, n), t)
    return pl.pallas_call(
        back_kernel,
        grid=(tokens // ROWS,),
        out_shape=(
            shape(ff, bf16),
            shape(width, f32),
            shape(width, bf16),
            shape(width, bf16),
            jax.ShapeDtypeStruct((8, width), f32),
        ),
        in_specs=[tok(width), tok(width), tok(ff), tok(width), tok(128), ANY, ANY, ANY]
        + [pl.BlockSpec((1, width), lambda i: (0, 0))],
        out_specs=(tok(ff), tok(width), tok(width), tok(width), pl.BlockSpec((8, width), lambda i: (0, 0))),
        scratch_shapes=[
            pltpu.VMEM((ff, width), bf16),
            pltpu.VMEM((width, ff), bf16),
            pltpu.VMEM((width, width), bf16),
            pltpu.SemaphoreType.DMA((3,)),
        ],
        compiler_params=params(dimension_semantics=("arbitrary",)),
        cost_estimate=cost(2 * tokens * width * (width + 2 * ff), 30 * tokens * width),
        name="back",
    )(d_two, d_down, slope, xhat1, rstd1, wd, wu, wo, g1)


def up_grad_kernel(place, mid_low, d_up, send, keep, buf, gsems):
    tokens, width = mid_low.shape
    size = width // 2

    def block(part):
        a = mid_low[:, pl.ds(pl.multiple_of((part & 1) * size, size), size)]
        b = d_up[:, pl.ds(pl.multiple_of((part >> 1) * width, width), width)]
        return mm_tn(a, b)

    write_group(block, send, keep, buf, gsems, place)


def up_grad(place, mid_low, d_up):
    tokens, width = mid_low.shape
    ff = d_up.shape[1]
    return pl.pallas_call(
        up_grad_kernel,
        out_shape=group_shapes(ff, width),
        in_specs=[SMEM, VMEM, VMEM],
        out_specs=(ANY, ANY),
        scratch_shapes=group_scratch(ff, width),
        compiler_params=params(),
        cost_estimate=cost(2 * tokens * width * ff, 14 * tokens * width),
        name="up_grad",
    )(place, mid_low, d_up)


def rest_grad_kernel(place, attn, x, d_branch, dq, dk, dv, vec, send, keep, lhs, rhs, buf, gsems, sems):
    tokens, width = x.shape
    size = width // 2
    pairs = [(attn, lhs.at[0]), (d_branch, rhs.at[0]), (x, lhs.at[1]), (dq, rhs.at[1]), (dk, rhs.at[2]), (dv, rhs.at[3])]
    copies = [pltpu.make_async_copy(a, b, sems.at[i]) for i, (a, b) in enumerate(pairs)]
    for c in copies:
        c.start()
    for c in copies:
        c.wait()
    ones = jnp.ones((8, tokens), bf16)
    vec[0:1, :] = mm(ones, rhs[1])[0:1]
    vec[1:2, :] = mm(ones, rhs[3])[0:1]
    vec[2:8, :] = jnp.zeros((6, width), f32)

    def block(part):
        which = part >> 1
        a = lhs[jnp.minimum(which, 1), :, pl.ds(pl.multiple_of((part & 1) * size, size), size)]
        return mm_tn(a, rhs[which])

    write_group(block, send, keep, buf, gsems, place)


def rest_grad(place, attn, x, d_branch, dq, dk, dv):
    tokens, width = x.shape
    rows = 4 * width
    return pl.pallas_call(
        rest_grad_kernel,
        out_shape=(jax.ShapeDtypeStruct((8, width), f32),) + group_shapes(rows, width),
        in_specs=[SMEM] + [ANY] * 6,
        out_specs=(VMEM, ANY, ANY),
        scratch_shapes=[pltpu.VMEM((2, tokens, width), bf16), pltpu.VMEM((4, tokens, width), bf16)]
        + group_scratch(rows, width)
        + [pltpu.SemaphoreType.DMA((6,))],
        compiler_params=params(),
        cost_estimate=cost(8 * tokens * width * width, 20 * tokens * width),
        name="rest_grad",
    )(place, attn, x, d_branch, dq, dk, dv)


def inputs_grad_kernel(d_one, dq, dk, dv, wq, wk, wv, out):
    out[...] = d_one[...] + mm_nt(dq[...], wq[...]) + mm_nt(dk[...], wk[...]) + mm_nt(dv[...], wv[...])


def inputs_grad(d_one, dq, dk, dv, wq, wk, wv):
    tokens, width = d_one.shape
    tok = pl.BlockSpec((ROWS, width), lambda i: (i, 0))
    full = pl.BlockSpec((width, width), lambda i: (0, 0))
    return pl.pallas_call(
        inputs_grad_kernel,
        grid=(tokens // ROWS,),
        out_shape=jax.ShapeDtypeStruct((tokens, width), f32),
        in_specs=[tok] * 4 + [full] * 3,
        out_specs=tok,
        compiler_params=params(dimension_semantics=("arbitrary",)),
        cost_estimate=cost(6 * tokens * width * width, 20 * tokens * width),
        name="inputs_grad",
    )(d_one, dq, dk, dv, wq, wk, wv)


def swap(value, axis, bit):
    count = lax.axis_size(axis)
    return lax.ppermute(value, axis, [(i, i ^ bit) for i in range(count)])


def plus(a, b):
    return (a.astype(f32) + b.astype(f32)).astype(bf16)


def layer_bits():
    return list(range(1, lax.axis_size("dp")))


def far_bits():
    bit, bits = PARTS, []
    while bit < lax.axis_size("seq"):
        bits.append(bit)
        bit *= 2
    return bits


def scatter_sum(send, keep):
    width = send.shape[-1]
    layers = lax.axis_size("dp")
    shape = (2, 2, 2, layers, send.shape[0] // (8 * layers), width)
    got = swap(send, "seq", 1)
    both = plus(keep, got).reshape(shape)
    a, b = both[0], both[1]
    ra, rb = swap(a[1], "seq", 2), swap(b[1], "seq", 4)
    a, b = plus(a[0], ra), plus(b[0], rb)
    ra, rb = swap(a[1], "seq", 4), swap(b[1], "seq", 2)
    a, b = plus(a[0], ra), plus(b[0], rb)
    both = jnp.stack([a, b], axis=1)
    terms = [both[0].astype(f32)] + [swap(both[d], "dp", d).astype(f32) for d in layer_bits()]
    while len(terms) > 1:
        terms = [terms[i] + terms[i + 1] for i in range(0, len(terms), 2)]
    total = terms[0].astype(bf16)
    for bit in far_bits():
        total = plus(total, swap(total, "seq", bit))
    return total


def gather_all(total):
    both = jnp.stack([total] + [swap(total, "dp", d) for d in layer_bits()], axis=0)
    a, b = both[:, 0], both[:, 1]
    a, b = jnp.stack([a, swap(a, "seq", 4)]), jnp.stack([b, swap(b, "seq", 2)])
    a, b = jnp.stack([a, swap(a, "seq", 2)]), jnp.stack([b, swap(b, "seq", 4)])
    mine = jnp.stack([a, b])
    mine = mine.reshape(8, -1, mine.shape[-1])
    return mine, swap(mine, "seq", 1)


def spread_kernel(kind, place, ma, mb, oa, ob, *refs):
    outs, (buf, sems) = refs[:-2], refs[-2:]
    j = pl.program_id(0)
    here, layer = place[1], place[2]
    half = ma.shape[1]
    size = 2 * half
    layers = LAYERS[0]
    chunk = half // layers
    width = ma.shape[2]

    def copies(step):
        part = step ^ here
        slot = step & 1
        src = buf.at[slot]
        if kind == "down":
            return [(None, pltpu.make_async_copy(src, outs[0].at[pl.ds(pl.multiple_of(part * size, size), size)], sems.at[slot]))]
        at = pl.ds(pl.multiple_of((part & 1) * size, size), size)
        which = part >> 1
        if kind == "up":
            cols = pl.ds(pl.multiple_of(which * width, width), width)
            return [(None, pltpu.make_async_copy(src, outs[0].at[at, cols], sems.at[slot]))]
        return [(which == n, pltpu.make_async_copy(src, o.at[at], sems.at[slot])) for n, o in enumerate(outs)]

    def start(step):
        for cond, c in copies(step):
            if cond is None:
                c.start()
            else:
                pl.when(cond)(c.start)

    def wait(step):
        copies(step)[0][1].wait()

    pl.when(j >= 2)(lambda: wait(j - 2))
    slot = j & 1

    def fill(a, b):
        for z in range(layers):
            to = (z ^ layer) * chunk
            rows = slice(z * chunk, (z + 1) * chunk)
            buf[slot, pl.ds(pl.multiple_of(to, chunk), chunk), :] = a[0, rows, :].astype(f32)
            buf[slot, pl.ds(pl.multiple_of(half + to, chunk), chunk), :] = b[0, rows, :].astype(f32)

    pl.when((j & 1) == 0)(lambda: fill(ma, mb))
    pl.when((j & 1) == 1)(lambda: fill(oa, ob))
    start(j)

    @pl.when(j == PARTS - 1)
    def _():
        wait(j - 1)
        wait(j)


def spread(kind, place, mine, other):
    half, width = mine.shape[1:]
    rows = 2 * half * PARTS
    a = pl.BlockSpec((1, half, width), lambda j: (2 * ((j >> 1) & 1) + (j >> 2), 0, 0))
    b = pl.BlockSpec((1, half, width), lambda j: (4 + 2 * (j >> 2) + ((j >> 1) & 1), 0, 0))
    if kind == "down":
        shapes = [(rows, width)]
    elif kind == "up":
        shapes = [(width, rows)]
    else:
        shapes = [(width, width)] * 4
    return pl.pallas_call(
        functools.partial(spread_kernel, kind),
        grid=(PARTS,),
        out_shape=[jax.ShapeDtypeStruct(s, f32) for s in shapes],
        in_specs=[SMEM, a, b, a, b],
        out_specs=[ANY] * len(shapes),
        scratch_shapes=[pltpu.VMEM((2, 2 * half, width), f32), pltpu.SemaphoreType.DMA((2,))],
        compiler_params=params(dimension_semantics=("arbitrary",)),
        cost_estimate=cost(rows * width, 6 * rows * width),
        name="spread_" + kind,
    )(place, mine, mine, other, other)


def sum_small(vec):
    for axis in ("seq", "dp"):
        bit = 1
        while bit < lax.axis_size(axis):
            vec = vec + swap(vec, axis, bit)
            bit *= 2
    return vec


def neighbours(value, reach):
    count = lax.axis_size("seq")
    up = [(i, i + 1) for i in range(count - 1)]
    low = lax.ppermute(value[-reach:], "seq", up)
    high = lax.ppermute(value[:reach], "seq", [(b, a) for a, b in up])
    return low, high


def body(
    inputs, lengths, w_query, b_query, w_key, w_value, b_value, w_out, b_out, gain_one, shift_one,
    w_up, b_up, w_down, b_down, gain_two, shift_two, d_output,
):
    rows, tokens, width = inputs.shape
    reach = ITEM_MOST
    LAYERS[0] = lax.axis_size("dp")
    here = lax.axis_index("seq")
    place = jnp.stack([here * tokens, here & (PARTS - 1), lax.axis_index("dp")]).astype(i32)
    x = inputs.reshape(tokens, width)
    dy = d_output.reshape(tokens, width)
    line = lambda v: v.reshape(1, -1)

    xl, xr = neighbours(x, reach)
    q, k, v, se, spans = front(place, lengths, x, w_query, w_key, w_value, line(b_query), line(b_value), reach)
    attn, kh, vh = attend(spans, se, q, k, v, xl, xr, w_key, w_value, line(b_value))
    output, slope, mid_low, xhat1, rstd1, d_two, d_down, vec_a, send1, keep1 = chain(
        place, spans, attn, x, dy, w_out, w_up, w_down, line(b_out), line(gain_one), line(shift_one),
        line(b_up), line(b_down), line(gain_two), line(shift_two),
    )
    d_up, d_one, d_branch, d_attn, vec_b = back(
        d_two, d_down, slope, xhat1, rstd1, w_down, w_up, w_out, line(gain_one)
    )
    dl, dr = neighbours(d_attn, reach)
    send2, keep2 = up_grad(place, mid_low, d_up)
    dq, dk, dv = attend_back(spans, se, q, k, v, d_attn, kh, vh, xl, xr, dl, dr, w_query, line(b_query))
    vec_c, send3, keep3 = rest_grad(place, attn, x, d_branch, dq, dk, dv)
    d_inputs = inputs_grad(d_one, dq, dk, dv, w_query, w_key, w_value)

    (g_w_down,) = spread("down", place, *gather_all(scatter_sum(send1, keep1)))
    (g_w_up,) = spread("up", place, *gather_all(scatter_sum(send2, keep2)))
    g_w_out, g_w_query, g_w_key, g_w_value = spread("rest", place, *gather_all(scatter_sum(send3, keep3)))
    small = sum_small(jnp.concatenate([vec_a, vec_b, vec_c], axis=0))
    ff = w_up.shape[1]
    many = ff // width
    return (
        output.reshape(rows, tokens, width),
        d_inputs.reshape(rows, tokens, width),
        g_w_query,
        small[16],
        g_w_key,
        g_w_value,
        small[17],
        g_w_out,
        small[10],
        small[8],
        small[9],
        g_w_up,
        small[11 : 11 + many].reshape(ff),
        g_w_down,
        small[0],
        small[1],
        small[2],
    )


def solution(mesh):
    split, whole = P("dp", "seq", None), P()
    return jax.shard_map(
        body,
        mesh=mesh,
        in_specs=(split, P("dp", None)) + (whole,) * 15 + (split,),
        out_specs=(split, split) + (whole,) * 15,
        check_vma=False,
    )
```

time: 1070 us -> 422 us (0.39)
  waiting for transfers between devices: 383 us -> 105 us
  matrix products: 258 us -> 0 us
  local copies, waits for them, and re-layouts: 221 us -> 10.9 us
  Pallas kernels: 0 us -> 176 us
  other arithmetic: 118 us -> 11.2 us
  starting transfers between devices: 10.6 us -> 111 us
  blocking collectives: 52.4 us -> 0 us
  between operations: 15.1 us -> 1.7 us
    psum x1 -> x0, waiting for transfers between devices: 383 us -> none  [body(): lax.psum((g_w_query, g_b_query, g_w_key, g_w_value, g_b_value, g_w_out, g...]
    dot_general x29 -> x0, matrix products: 258 us -> none  [the longest x4 53.3 us: block_scores(): jnp.einsum('qhd,khd->hqk', query_h, key_h, preferred_element_type=jnp.flo...]
    pallas_call x0 -> x11, Pallas kernels: none -> 176 us  [the longest x1 40.3 us: attend_back(): pl.pallas_call(attend_back_kernel, out_shape=(out, out, out), in_specs=[S...]
    gather x20 -> x0, local copies, waits for them, and re-layouts: 129 us -> none  [segment_ids(): return jnp.searchsorted(ends, positions, side='right')]
    ppermute x4 -> x57, waiting for transfers between devices: 0.01 us -> 105 us  [the longest x53 105 us: swap(): return lax.ppermute(value, axis, [(i, i ^ bit) for i in range(count)])]
    ppermute x4 -> x57, starting transfers between devices: 10.5 us -> 111 us  [the longest x53 101 us: swap(): return lax.ppermute(value, axis, [(i, i ^ bit) for i in range(count)])]
    psum x1 -> x0, blocking collectives: 52.4 us -> none  [body(): lax.psum((g_w_query, g_b_query, g_w_key, g_w_value, g_b_value, g_w_out, g...]
    unnamed x134 -> x38, local copies, waits for them, and re-layouts: 41.7 us -> 1.81 us
  transfers between devices with their start and end apart: 5 -> 57, of which waited for: 1 -> 22; matrix products, arithmetic and copies ran while one was open for 22% -> 4% of each run, Pallas kernels for 0% -> 23%
where the time goes in v1:
time: 422 us; the launch traced here: 416 us
  Pallas kernels  176 us (42%)
  starting transfers between devices  111 us (26%)
  waiting for transfers between devices  105 us (25%)
  other arithmetic  11.2 us (3%)
  local copies, waits for them, and re-layouts  10.9 us (3%)
    ppermute x53, waiting for transfers between devices, swap(): return lax.ppermute(value, axis, [(i, i ^ bit) for i in range(count)])  105 us
    ppermute x53, starting transfers between devices, swap(): return lax.ppermute(value, axis, [(i, i ^ bit) for i in range(count)])  101 us
    pallas_call x1, Pallas kernels, attend_back(): pl.pallas_call(attend_back_kernel, out_shape=(out, out, out), in_specs=[S...  40.3 us
    pallas_call x1, Pallas kernels, chain(): pl.pallas_call(chain_kernel, grid=(tokens // ROWS,), out_shape=(shape(wid...  34 us
    pallas_call x3, Pallas kernels, spread(): pl.pallas_call(functools.partial(spread_kernel, kind), grid=(PARTS,), out...  28.1 us
    pallas_call x1, Pallas kernels, attend(): pl.pallas_call(attend_kernel, out_shape=(jax.ShapeDtypeStruct((tokens, wi...  18.2 us
    pallas_call x1, Pallas kernels, back(): pl.pallas_call(back_kernel, grid=(tokens // ROWS,), out_shape=(shape(ff,...  18 us
    pallas_call x1, Pallas kernels, rest_grad(): pl.pallas_call(rest_grad_kernel, out_shape=(jax.ShapeDtypeStruct((8, widt...  11.5 us
  transfers between devices with their start and end apart: 57, of which 22 were waited for; matrix products, arithmetic and copies ran while one was open for 4% of the time, Pallas kernels for 23%

profile of v1, /device:TPU:0, one launch (start us, length us, event | category | flops | bytes accessed | tf_op | source)
XLA Modules:
  0.0 415.5 jit_solution(6270726198478008859)
XLA Ops:
  10.9 8.8 %front.1 = (bf16[768,768]{1,0:T(8,128)(2,1)}, bf16[768,768]{1,0:T(8,128)(2,1)}, bf16[768,768]{1,0:T(8,128)(2,1)}, f32[8,1280]{1,0:T(8,128)}, s32[28]{0:T(128)}) custom-call(s32[3]{0:T(128)} %pad_add_fusion.place, s32[1,784]{1,0:T(1,128)} %lengths.1, bf16[768,768]{1,0:T(8,128)(2,1)} %bitcast.235, bf16[768,768]{1,0:T(8,128)(2,1)} %wq.5, bf16[768,768]{1,0:T(8,128)(2,1)} %wk.5, ...), custom_call_target="tpu_custom_call" | custom-call | flops 2717908992 | bytes 4718592 | tf_op jit(solution)/shard_map/front/pallas_call | solution.py:133
  20.6 18.2 %attend.1 = (bf16[768,768]{1,0:T(8,128)(2,1)}, bf16[512,768]{1,0:T(8,128)(2,1)}, bf16[512,768]{1,0:T(8,128)(2,1)}) custom-call(s32[28]{0:T(128)} %get-tuple-element.52.spans, f32[8,1280]{1,0:T(8,128)} %get-tuple-element.53.se, bf16[768,768]{1,0:T(8,128)(2,1)} %get-tuple-element.54.q, bf16[768,768]{1,0:T(8,128)(2,1)} %get-tuple-element.55.k, ...), custom_call_target="tpu_custom_call" | custom-call | flops 8000000000 | bytes 7077888 | tf_op jit(solution)/shard_map/attend/pallas_call | solution.py:225
  38.8 34.0 %chain.1 = (bf16[768,768]{1,0:T(8,128)(2,1)}, bf16[768,3072]{1,0:T(8,128)(2,1)}, bf16[768,768]{1,0:T(8,128)(2,1)}, f32[768,768]{1,0:T(8,128)}, f32[768,128]{1,0:...) custom-call(s32[3]{0:T(128)} %pad_add_fusion.place, ...), custom_call_target="tpu_custom_call" | custom-call | flops 11777605632 | bytes 17694720 | tf_op jit(solution)/shard_map/chain/pallas_call | solution.py:498
  72.8 18.0 %back.1 = (bf16[768,3072]{1,0:T(8,128)(2,1)}, f32[768,768]{1,0:T(8,128)}, bf16[768,768]{1,0:T(8,128)(2,1)}, bf16[768,768]{1,0:T(8,128)(2,1)}, f32[8,768]{1,0:T(8,128)}) custom-call(f32[768,768]{1,0:T(8,128)} %get-tuple-element.59.d_two, bf16[768,768]{1,0:T(8,128)(2,1)} %get-tuple-element.60.d_down, bf16[768,3072]{1,0:T(8,128)(2,1)} %get-tuple-element.61.slope, ...), custom_call_target="tpu_custom_call" | custom-call | flops 8153726976 | bytes 17694720 | tf_op jit(solution)/shard_map/back/pallas_call | solution.py:586
  92.0 4.7 %collective-permute-start.2 = (bf16[256,768]{1,0:T(8,128)(2,1)S(1)}, bf16[256,768]{1,0:T(8,128)(2,1)S(1)}, u32[]{:S(2)}, u32[]{:S(2)}) collective-permute-start(bf16[256,768]{1,0:T(8,128)(2,1)S(1)} %get-tuple-element.108), channel_id=1, source_target_pairs={{0,1},{1,2},{2,3},{3,4},{4,5},{5,6},{6,7},{8,9},{9,10},{10,11},{11... | collective-permute-start | bytes 1179656 | tf_op jit(solution)/shard_map/ppermute | solution.py:838
  98.0 9.4 %up_grad.1 = (bf16[1536,768]{1,0:T(8,128)(2,1)}, bf16[1536,768]{1,0:T(8,128)(2,1)}) custom-call(s32[3]{0:T(128)} %pad_add_fusion.place, bf16[768,768]{1,0:T(8,128)(2,1)} %get-tuple-element.81.mid_low, bf16[768,3072]{1,0:T(8,128)(2,1)} %get-tuple-element.82.d_up), custom_call_target="tpu_custom_call" | custom-call | flops 3623878656 | bytes 8257536 | tf_op jit(solution)/shard_map/up_grad/pallas_call | solution.py:626
  110.8 40.3 %attend_back.1 = (bf16[768,768]{1,0:T(8,128)(2,1)}, bf16[768,768]{1,0:T(8,128)(2,1)}, bf16[768,768]{1,0:T(8,128)(2,1)}) custom-call(s32[28]{0:T(128)} %get-tuple-element.52.spans, f32[8,1280]{1,0:T(8,128)} %get-tuple-element.53.se, bf16[768,768]{1,0:T(8,128)(2,1)} %get-tuple-element.54.q, bf16[768,768]{1,0:T(8,128)(2,1)} %get-tuple-element.55.k, ...), custom_call_target="tpu_custom_call" | custom-call | flops 16000000000 | bytes 11796480 | tf_op jit(solution)/shard_map/attend_back/pallas_call | solution.py:315
  151.1 11.5 %rest_grad.1 = (f32[8,768]{1,0:T(8,128)}, bf16[1536,768]{1,0:T(8,128)(2,1)}, bf16[1536,768]{1,0:T(8,128)(2,1)}) custom-call(s32[3]{0:T(128)} %pad_add_fusion.place, bf16[768,768]{1,0:T(8,128)(2,1)} %get-tuple-element.57.attn, bf16[768,768]{1,0:T(8,128)(2,1)} %bitcast.237, bf16[768,768]{1,0:T(8,128)(2,1)} %get-tuple-element.71.d_branch, ...), custom_call_target="tpu_custom_call" | custom-call | flops 3623878656 | bytes 11796480 | tf_op jit(solution)/shard_map/rest_grad/pallas_call | solution.py:663
  171.1 11.5 %collective-permute-start.28 = (bf16[2,4,48,768]{3,2,1,0:T(8,128)(2,1)S(1)}, bf16[2,4,48,768]{3,2,1,0:T(8,128)(2,1)S(1)}, u32[]{:S(2)}, u32[]{:S(2)}) collective-permute-start(bf16[2,4,48,768]{3,2,1,0:T(8,128)(2,1)S(1)} %bitcast.223), channel_id=1, source_target_pairs={{0,4},{1,5},{2,6},{3,7},{4,0},{5,1},{6,2},{7,3},{8,12},{9,13},{10,... | collective-permute-start | bytes 1769480 | tf_op jit(solution)/shard_map/ppermute | solution.py:699
  186.3 10.5 %collective-permute-start.7 = (bf16[2,4,48,768]{3,2,1,0:T(8,128)(2,1)S(1)}, bf16[2,4,48,768]{3,2,1,0:T(8,128)(2,1)S(1)}, u32[]{:S(2)}, u32[]{:S(2)}) collective-permute-start(bf16[2,4,48,768]{3,2,1,0:T(8,128)(2,1)S(1)} %bitcast.220), channel_id=1, source_target_pairs={{0,4},{1,5},{2,6},{3,7},{4,0},{5,1},{6,2},{7,3},{8,12},{9,13},{10,... | collective-permute-start | bytes 1769480 | tf_op jit(solution)/shard_map/ppermute | solution.py:699
  199.8 9.5 %collective-permute-done.44 = bf16[2,4,48,768]{3,2,1,0:T(8,128)(2,1)S(1)} collective-permute-done((bf16[2,4,48,768]{3,2,1,0:T(8,128)(2,1)S(1)}, bf16[2,4,48,768]{3,2,1,0:T(8,128)(2,1)S(1)}, u32[]{:S(2)}, u32[]{:S(2)}) %collective-permute-start.44) | collective-permute-done | bytes 589856 | tf_op jit(solution)/shard_map/ppermute | solution.py:699
  211.7 16.5 %collective-permute-done.27 = bf16[4,48,768]{2,1,0:T(8,128)(2,1)S(1)} collective-permute-done((bf16[4,48,768]{2,1,0:T(8,128)(2,1)S(1)}, bf16[4,48,768]{2,1,0:T(8,128)(2,1)S(1)}, u32[]{:S(2)}, u32[]{:S(2)}) %collective-permute-start.27) | collective-permute-done | bytes 294944 | tf_op jit(solution)/shard_map/ppermute | solution.py:699
  234.2 6.5 %collective-permute-start.31 = (bf16[2,48,768]{2,1,0:T(8,128)(2,1)S(1)}, bf16[2,48,768]{2,1,0:T(8,128)(2,1)S(1)}, u32[]{:S(2)}, u32[]{:S(2)}) collective-permute-start(bf16[2,48,768]{2,1,0:T(8,128)(2,1)S(1)} %get-tuple-element.132), channel_id=1, source_target_pairs={{0,16},{8,24},{16,0},{24,8},{1,17},{9,25},{17,1},{25,9},{2,18},{10... | collective-permute-start | bytes 442376 | tf_op jit(solution)/shard_map/ppermute | solution.py:699
  259.8 7.2 %collective-permute-start.33 = (bf16[2,48,768]{2,1,0:T(8,128)(2,1)S(1)}, bf16[2,48,768]{2,1,0:T(8,128)(2,1)S(1)}, u32[]{:S(2)}, u32[]{:S(2)}) collective-permute-start(bf16[2,48,768]{2,1,0:T(8,128)(2,1)S(1)} %fusion.21), channel_id=1, source_target_pairs={{0,8},{8,0},{16,24},{24,16},{1,9},{9,1},{17,25},{25,17},{2,10},{10... | collective-permute-start | bytes 442376 | tf_op jit(solution)/shard_map/ppermute | solution.py:699
  267.1 5.3 %collective-permute-done.34 = bf16[2,48,768]{2,1,0:T(8,128)(2,1)S(1)} collective-permute-done((bf16[2,48,768]{2,1,0:T(8,128)(2,1)S(1)}, bf16[2,48,768]{2,1,0:T(8,128)(2,1)S(1)}, u32[]{:S(2)}, u32[]{:S(2)}) %collective-permute-start.34) | collective-permute-done | bytes 147488 | tf_op jit(solution)/shard_map/ppermute | solution.py:699
  272.5 7.1 %collective-permute-start.49 = (bf16[2,48,768]{2,1,0:T(8,128)(2,1)S(1)}, bf16[2,48,768]{2,1,0:T(8,128)(2,1)S(1)}, u32[]{:S(2)}, u32[]{:S(2)}) collective-permute-start(bf16[2,48,768]{2,1,0:T(8,128)(2,1)S(1)} %fusion.19), channel_id=1, source_target_pairs={{0,8},{8,0},{16,24},{24,16},{1,9},{9,1},{17,25},{25,17},{2,10},{10... | collective-permute-start | bytes 442376 | tf_op jit(solution)/shard_map/ppermute | solution.py:699
  315.9 5.5 %collective-permute-done.17 = bf16[4,48,768]{2,1,0:T(8,128)(2,1)S(1)} collective-permute-done((bf16[4,48,768]{2,1,0:T(8,128)(2,1)S(1)}, bf16[4,48,768]{2,1,0:T(8,128)(2,1)S(1)}, u32[]{:S(2)}, u32[]{:S(2)}) %collective-permute-start.17) | collective-permute-done | bytes 294944 | tf_op jit(solution)/shard_map/ppermute | solution.py:699
  322.5 9.7 %collective-permute-done.15 = bf16[4,48,768]{2,1,0:T(8,128)(2,1)S(1)} collective-permute-done((bf16[4,48,768]{2,1,0:T(8,128)(2,1)S(1)}, bf16[4,48,768]{2,1,0:T(8,128)(2,1)S(1)}, u32[]{:S(2)}, u32[]{:S(2)}) %collective-permute-start.15) | collective-permute-done | bytes 294944 | tf_op jit(solution)/shard_map/ppermute | solution.py:699
  335.5 9.3 %collective-permute-done.55 = bf16[2,4,48,768]{3,2,1,0:T(8,128)(2,1)S(1)} collective-permute-done((bf16[2,4,48,768]{3,2,1,0:T(8,128)(2,1)S(1)}, bf16[2,4,48,768]{3,2,1,0:T(8,128)(2,1)S(1)}, u32[]{:S(2)}, u32[]{:S(2)}) %collective-permute-start.55) | collective-permute-done | bytes 589856 | tf_op jit(solution)/shard_map/ppermute | solution.py:699
  348.4 8.1 %collective-permute-done.18 = bf16[2,4,48,768]{3,2,1,0:T(8,128)(2,1)S(1)} collective-permute-done((bf16[2,4,48,768]{3,2,1,0:T(8,128)(2,1)S(1)}, bf16[2,4,48,768]{3,2,1,0:T(8,128)(2,1)S(1)}, u32[]{:S(2)}, u32[]{:S(2)}) %collective-permute-start.18) | collective-permute-done | bytes 589856 | tf_op jit(solution)/shard_map/ppermute | solution.py:699
  378.3 7.6 %inputs_grad.1 = f32[768,768]{1,0:T(8,128)} custom-call(f32[768,768]{1,0:T(8,128)} %get-tuple-element.64.d_one, bf16[768,768]{1,0:T(8,128)(2,1)} %get-tuple-element.68.dq, bf16[768,768]{1,0:T(8,128)(2,1)} %get-tuple-element.69.dk, bf16[768,768]{1,0:T(8,128)(2,1)} %get-tuple-element.70.dv, bf16[768,768]{1,0:T(8,128)(2,1)} %wq.5, bf16[768,768]{1,0:T(8,128)(2,1)} %wk.5, ...), custom_call_target="tpu_custom_call" | custom-call | flops 2717908992 | bytes 11796480 | tf_op jit(solution)/shard_map/inputs_grad/pallas_call | solution.py:685
  387.2 9.3 %spread_up.1 = f32[768,3072]{1,0:T(8,128)} custom-call(s32[3]{0:T(128)} %pad_add_fusion.place, bf16[8,192,768]{2,1,0:T(8,128)(2,1)} %bitcast.211, bf16[8,192,768]{2,1,0:T(8,128)(2,1)} %bitcast.212, bf16[8,192,768]{2,1,0:T(8,128)(2,1)} %collective-permute-done.40.oa.ob, bf16[8,192,768]{2,1,0:T(8,128)(2,1)} %collective-permute-done.40.oa.ob), custom_call_target="tpu_custom_call" | custom-call | flops 2359296 | bytes 14155776 | tf_op jit(solution)/shard_map/spread_up/pallas_call | solution.py:813
  396.6 9.4 %spread_down.1 = f32[3072,768]{1,0:T(8,128)} custom-call(s32[3]{0:T(128)} %pad_add_fusion.place, bf16[8,192,768]{2,1,0:T(8,128)(2,1)} %bitcast.111.ma.mb, bf16[8,192,768]{2,1,0:T(8,128)(2,1)} %bitcast.111.ma.mb, bf16[8,192,768]{2,1,0:T(8,128)(2,1)} %collective-permute-done.56.oa.ob, bf16[8,192,768]{2,1,0:T(8,128)(2,1)} %collective-permute-done.56.oa.ob), custom_call_target="tpu_custom_call" | custom-call | flops 2359296 | bytes 14155776 | tf_op jit(solution)/shard_map/spread_down/pallas_call | solution.py:813
  405.9 9.4 %spread_rest.1 = (f32[768,768]{1,0:T(8,128)}, f32[768,768]{1,0:T(8,128)}, f32[768,768]{1,0:T(8,128)}, f32[768,768]{1,0:T(8,128)}) custom-call(s32[3]{0:T(128)} %pad_add_fusion.place, bf16[8,192,768]{2,1,0:T(8,128)(2,1)} %bitcast.43.ma.mb, bf16[8,192,768]{2,1,0:T(8,128)(2,1)} %bitcast.43.ma.mb, bf16[8,192,768]{2,1,0:T(8,128)(2,1)} %collective-permute-done.19.oa.ob, ...), custom_call_target="tpu_custom_call" | custom-call | flops 2359296 | bytes 14155776 | tf_op jit(solution)/shard_map/spread_rest/pallas_call | solution.py:813
  (210 shorter events, 126.7 us)
Async XLA Ops:
  107.4 58.1 %collective-permute-start.25 = (bf16[1536,768]{1,0:T(8,128)(2,1)}, bf16[1536,768]{1,0:T(8,128)(2,1)}, u32[]{:S(2)}, u32[]{:S(2)}) collective-permute-start(bf16[1536,768]{1,0:T(8,128)(2,1)} %get-tuple-element.84), channel_id=1, source_target_pairs={{0,1},{1,0},{2,3},{3,2},{4,5},{5,4},{6,7},{7,6},{8,9},{9,8},{10,11... | collective-permute-start | bytes 7077896 | tf_op jit(solution)/shard_map/ppermute | solution.py:699
  109.8 72.8 %collective-permute-start.41 = (bf16[1536,768]{1,0:T(8,128)(2,1)}, bf16[1536,768]{1,0:T(8,128)(2,1)S(1)}, u32[]{:S(2)}, u32[]{:S(2)}) collective-permute-start(bf16[1536,768]{1,0:T(8,128)(2,1)} %get-tuple-element.86), channel_id=1, source_target_pairs={{0,1},{1,0},{2,3},{3,2},{4,5},{5,4},{6,7},{7,6},{8,9},{9,8},{10,11... | collective-permute-start | bytes 7077896 | tf_op jit(solution)/shard_map/ppermute | solution.py:699
  162.6 22.2 %collective-permute-start.4 = (bf16[1536,768]{1,0:T(8,128)(2,1)}, bf16[1536,768]{1,0:T(8,128)(2,1)S(1)}, u32[]{:S(2)}, u32[]{:S(2)}) collective-permute-start(bf16[1536,768]{1,0:T(8,128)(2,1)} %get-tuple-element.73), channel_id=1, source_target_pairs={{0,1},{1,0},{2,3},{3,2},{4,5},{5,4},{6,7},{7,6},{8,9},{9,8},{10,11... | collective-permute-start | bytes 7077896 | tf_op jit(solution)/shard_map/ppermute | solution.py:699
  171.1 25.8 %collective-permute-start.28 = (bf16[2,4,48,768]{3,2,1,0:T(8,128)(2,1)S(1)}, bf16[2,4,48,768]{3,2,1,0:T(8,128)(2,1)S(1)}, u32[]{:S(2)}, u32[]{:S(2)}) collective-permute-start(bf16[2,4,48,768]{3,2,1,0:T(8,128)(2,1)S(1)} %bitcast.223), channel_id=1, source_target_pairs={{0,4},{1,5},{2,6},{3,7},{4,0},{5,1},{6,2},{7,3},{8,12},{9,13},{10,... | collective-permute-start | bytes 1769480 | tf_op jit(solution)/shard_map/ppermute | solution.py:699
  183.5 25.8 %collective-permute-start.44 = (bf16[2,4,48,768]{3,2,1,0:T(8,128)(2,1)S(1)}, bf16[2,4,48,768]{3,2,1,0:T(8,128)(2,1)S(1)}, u32[]{:S(2)}, u32[]{:S(2)}) collective-permute-start(bf16[2,4,48,768]{3,2,1,0:T(8,128)(2,1)S(1)} %bitcast.222), channel_id=1, source_target_pairs={{0,4},{1,5},{2,6},{3,7},{4,0},{5,1},{6,2},{7,3},{8,12},{9,13},{10,... | collective-permute-start | bytes 1769480 | tf_op jit(solution)/shard_map/ppermute | solution.py:699
  185.6 55.4 %collective-permute-start.5 = (bf16[2,4,48,768]{3,2,1,0:T(8,128)(2,1)S(1)}, bf16[2,4,48,768]{3,2,1,0:T(8,128)(2,1)S(1)}, u32[]{:S(2)}, u32[]{:S(2)}) collective-permute-start(bf16[2,4,48,768]{3,2,1,0:T(8,128)(2,1)S(1)} %bitcast.221), channel_id=1, source_target_pairs={{0,2},{1,3},{2,0},{3,1},{4,6},{5,7},{6,4},{7,5},{8,10},{9,11},{10,... | collective-permute-start | bytes 1769480 | tf_op jit(solution)/shard_map/ppermute | solution.py:699
  186.3 58.3 %collective-permute-start.7 = (bf16[2,4,48,768]{3,2,1,0:T(8,128)(2,1)S(1)}, bf16[2,4,48,768]{3,2,1,0:T(8,128)(2,1)S(1)}, u32[]{:S(2)}, u32[]{:S(2)}) collective-permute-start(bf16[2,4,48,768]{3,2,1,0:T(8,128)(2,1)S(1)} %bitcast.220), channel_id=1, source_target_pairs={{0,4},{1,5},{2,6},{3,7},{4,0},{5,1},{6,2},{7,3},{8,12},{9,13},{10,... | collective-permute-start | bytes 1769480 | tf_op jit(solution)/shard_map/ppermute | solution.py:699
  196.9 31.3 %collective-permute-start.27 = (bf16[4,48,768]{2,1,0:T(8,128)(2,1)S(1)}, bf16[4,48,768]{2,1,0:T(8,128)(2,1)S(1)}, u32[]{:S(2)}, u32[]{:S(2)}) collective-permute-start(bf16[4,48,768]{2,1,0:T(8,128)(2,1)S(1)} %slice_bitcast_fusion.8), channel_id=1, source_target_pairs={{0,4},{1,5},{2,6},{3,7},{4,0},{5,1},{6,2},{7,3},{8,12},{9,13},{10,... | collective-permute-start | bytes 884744 | tf_op jit(solution)/shard_map/ppermute | solution.py:699
  199.6 28.9 %collective-permute-start.29 = (bf16[4,48,768]{2,1,0:T(8,128)(2,1)S(1)}, bf16[4,48,768]{2,1,0:T(8,128)(2,1)S(1)}, u32[]{:S(2)}, u32[]{:S(2)}) collective-permute-start(bf16[4,48,768]{2,1,0:T(8,128)(2,1)S(1)} %slice_bitcast_fusion.6), channel_id=1, source_target_pairs={{0,2},{1,3},{2,0},{3,1},{4,6},{5,7},{6,4},{7,5},{8,10},{9,11},{10,... | collective-permute-start | bytes 884744 | tf_op jit(solution)/shard_map/ppermute | solution.py:699
  209.3 24.9 %collective-permute-start.43 = (bf16[4,48,768]{2,1,0:T(8,128)(2,1)S(1)}, bf16[4,48,768]{2,1,0:T(8,128)(2,1)S(1)}, u32[]{:S(2)}, u32[]{:S(2)}) collective-permute-start(bf16[4,48,768]{2,1,0:T(8,128)(2,1)S(1)} %slice_bitcast_fusion.4), channel_id=1, source_target_pairs={{0,4},{1,5},{2,6},{3,7},{4,0},{5,1},{6,2},{7,3},{8,12},{9,13},{10,... | collective-permute-start | bytes 884744 | tf_op jit(solution)/shard_map/ppermute | solution.py:699
  247.5 32.1 %collective-permute-start.6 = (bf16[4,48,768]{2,1,0:T(8,128)(2,1)S(1)}, bf16[4,48,768]{2,1,0:T(8,128)(2,1)S(1)}, u32[]{:S(2)}, u32[]{:S(2)}) collective-permute-start(bf16[4,48,768]{2,1,0:T(8,128)(2,1)S(1)} %slice_bitcast_fusion.12), channel_id=1, source_target_pairs={{0,4},{1,5},{2,6},{3,7},{4,0},{5,1},{6,2},{7,3},{8,12},{9,13},{10,... | collective-permute-start | bytes 884744 | tf_op jit(solution)/shard_map/ppermute | solution.py:699
  251.2 28.6 %collective-permute-start.8 = (bf16[4,48,768]{2,1,0:T(8,128)(2,1)S(1)}, bf16[4,48,768]{2,1,0:T(8,128)(2,1)S(1)}, u32[]{:S(2)}, u32[]{:S(2)}) collective-permute-start(bf16[4,48,768]{2,1,0:T(8,128)(2,1)S(1)} %slice_bitcast_fusion.10), channel_id=1, source_target_pairs={{0,2},{1,3},{2,0},{3,1},{4,6},{5,7},{6,4},{7,5},{8,10},{9,11},{10,... | collective-permute-start | bytes 884744 | tf_op jit(solution)/shard_map/ppermute | solution.py:699
  272.5 19.3 %collective-permute-start.49 = (bf16[2,48,768]{2,1,0:T(8,128)(2,1)S(1)}, bf16[2,48,768]{2,1,0:T(8,128)(2,1)S(1)}, u32[]{:S(2)}, u32[]{:S(2)}) collective-permute-start(bf16[2,48,768]{2,1,0:T(8,128)(2,1)S(1)} %fusion.19), channel_id=1, source_target_pairs={{0,8},{8,0},{16,24},{24,16},{1,9},{9,1},{17,25},{25,17},{2,10},{10... | collective-permute-start | bytes 442376 | tf_op jit(solution)/shard_map/ppermute | solution.py:699
  291.8 20.7 %collective-permute-start.36 = (bf16[4,48,768]{2,1,0:T(8,128)(2,1)S(1)}, bf16[4,48,768]{2,1,0:T(8,128)(2,1)S(1)}, u32[]{:S(2)}, u32[]{:S(2)}) collective-permute-start(bf16[4,48,768]{2,1,0:T(8,128)(2,1)S(1)} %get-tuple-element.125), channel_id=1, source_target_pairs={{0,4},{1,5},{2,6},{3,7},{4,0},{5,1},{6,2},{7,3},{8,12},{9,13},{10,... | collective-permute-start | bytes 884744 | tf_op jit(solution)/shard_map/ppermute | solution.py:699
  309.7 24.2 %collective-permute-start.39 = (bf16[2,4,48,768]{3,2,1,0:T(8,128)(2,1)S(1)}, bf16[2,4,48,768]{3,2,1,0:T(8,128)(2,1)S(1)}, u32[]{:S(2)}, u32[]{:S(2)}) collective-permute-start(bf16[2,4,48,768]{3,2,1,0:T(8,128)(2,1)S(1)} %get-tuple-element.129), channel_id=1, source_target_pairs={{0,4},{1,5},{2,6},{3,7},{4,0},{5,1},{6,2},{7,3},{8,12},{9,13},{10,... | collective-permute-start | bytes 1769480 | tf_op jit(solution)/shard_map/ppermute | solution.py:699
  312.6 22.4 %collective-permute-start.37 = (bf16[2,4,48,768]{3,2,1,0:T(8,128)(2,1)S(1)}, bf16[2,4,48,768]{3,2,1,0:T(8,128)(2,1)S(1)}, u32[]{:S(2)}, u32[]{:S(2)}) collective-permute-start(bf16[2,4,48,768]{3,2,1,0:T(8,128)(2,1)S(1)} %get-tuple-element.123), channel_id=1, source_target_pairs={{0,2},{1,3},{2,0},{3,1},{4,6},{5,7},{6,4},{7,5},{8,10},{9,11},{10,... | collective-permute-start | bytes 1769480 | tf_op jit(solution)/shard_map/ppermute | solution.py:699
  313.7 18.5 %collective-permute-start.15 = (bf16[4,48,768]{2,1,0:T(8,128)(2,1)S(1)}, bf16[4,48,768]{2,1,0:T(8,128)(2,1)S(1)}, u32[]{:S(2)}, u32[]{:S(2)}) collective-permute-start(bf16[4,48,768]{2,1,0:T(8,128)(2,1)S(1)} %get-tuple-element.136), channel_id=1, source_target_pairs={{0,4},{1,5},{2,6},{3,7},{4,0},{5,1},{6,2},{7,3},{8,12},{9,13},{10,... | collective-permute-start | bytes 884744 | tf_op jit(solution)/shard_map/ppermute | solution.py:699
  314.2 30.6 %collective-permute-start.55 = (bf16[2,4,48,768]{3,2,1,0:T(8,128)(2,1)S(1)}, bf16[2,4,48,768]{3,2,1,0:T(8,128)(2,1)S(1)}, u32[]{:S(2)}, u32[]{:S(2)}) collective-permute-start(bf16[2,4,48,768]{3,2,1,0:T(8,128)(2,1)S(1)} %get-tuple-element.118), channel_id=1, source_target_pairs={{0,4},{1,5},{2,6},{3,7},{4,0},{5,1},{6,2},{7,3},{8,12},{9,13},{10,... | collective-permute-start | bytes 1769480 | tf_op jit(solution)/shard_map/ppermute | solution.py:699
  321.4 25.3 %collective-permute-start.53 = (bf16[2,4,48,768]{3,2,1,0:T(8,128)(2,1)S(1)}, bf16[2,4,48,768]{3,2,1,0:T(8,128)(2,1)S(1)}, u32[]{:S(2)}, u32[]{:S(2)}) collective-permute-start(bf16[2,4,48,768]{3,2,1,0:T(8,128)(2,1)S(1)} %get-tuple-element.112), channel_id=1, source_target_pairs={{0,2},{1,3},{2,0},{3,1},{4,6},{5,7},{6,4},{7,5},{8,10},{9,11},{10,... | collective-permute-start | bytes 1769480 | tf_op jit(solution)/shard_map/ppermute | solution.py:699
  332.2 24.4 %collective-permute-start.18 = (bf16[2,4,48,768]{3,2,1,0:T(8,128)(2,1)S(1)}, bf16[2,4,48,768]{3,2,1,0:T(8,128)(2,1)S(1)}, u32[]{:S(2)}, u32[]{:S(2)}) collective-permute-start(bf16[2,4,48,768]{3,2,1,0:T(8,128)(2,1)S(1)} %get-tuple-element.140), channel_id=1, source_target_pairs={{0,4},{1,5},{2,6},{3,7},{4,0},{5,1},{6,2},{7,3},{8,12},{9,13},{10,... | collective-permute-start | bytes 1769480 | tf_op jit(solution)/shard_map/ppermute | solution.py:699
  333.9 24.0 %collective-permute-start.16 = (bf16[2,4,48,768]{3,2,1,0:T(8,128)(2,1)S(1)}, bf16[2,4,48,768]{3,2,1,0:T(8,128)(2,1)S(1)}, u32[]{:S(2)}, u32[]{:S(2)}) collective-permute-start(bf16[2,4,48,768]{3,2,1,0:T(8,128)(2,1)S(1)} %get-tuple-element.134), channel_id=1, source_target_pairs={{0,2},{1,3},{2,0},{3,1},{4,6},{5,7},{6,4},{7,5},{8,10},{9,11},{10,... | collective-permute-start | bytes 1769480 | tf_op jit(solution)/shard_map/ppermute | solution.py:699
  335.4 51.8 %collective-permute-start.40 = (bf16[8,192,768]{2,1,0:T(8,128)(2,1)S(1)}, bf16[8,192,768]{2,1,0:T(8,128)(2,1)}, u32[]{:S(2)}, u32[]{:S(2)}) collective-permute-start(bf16[8,192,768]{2,1,0:T(8,128)(2,1)S(1)} %bitcast.210), channel_id=1, source_target_pairs={{0,1},{1,0},{2,3},{3,2},{4,5},{5,4},{6,7},{7,6},{8,9},{9,8},{10,11... | collective-permute-start | bytes 7077896 | tf_op jit(solution)/shard_map/ppermute | solution.py:699
  348.4 48.1 %collective-permute-start.56 = (bf16[8,192,768]{2,1,0:T(8,128)(2,1)}, bf16[8,192,768]{2,1,0:T(8,128)(2,1)}, u32[]{:S(2)}, u32[]{:S(2)}) collective-permute-start(bf16[8,192,768]{2,1,0:T(8,128)(2,1)} %bitcast.111.ma.mb), channel_id=1, source_target_pairs={{0,1},{1,0},{2,3},{3,2},{4,5},{5,4},{6,7},{7,6},{8,9},{9,8},{10,11... | collective-permute-start | bytes 7077896 | tf_op jit(solution)/shard_map/ppermute | solution.py:699
  359.6 46.3 %collective-permute-start.19 = (bf16[8,192,768]{2,1,0:T(8,128)(2,1)}, bf16[8,192,768]{2,1,0:T(8,128)(2,1)}, u32[]{:S(2)}, u32[]{:S(2)}) collective-permute-start(bf16[8,192,768]{2,1,0:T(8,128)(2,1)} %bitcast.43.ma.mb), channel_id=1, source_target_pairs={{0,1},{1,0},{2,3},{3,2},{4,5},{5,4},{6,7},{7,6},{8,9},{9,8},{10,11... | collective-permute-start | bytes 7077896 | tf_op jit(solution)/shard_map/ppermute | solution.py:699
  (51 other events, 499.7 us)

commit v2 on v1

v2 whole, which is shorter than its diff:
```python
import functools

import jax
import jax.numpy as jnp
from jax import lax
from jax.experimental import pallas as pl
from jax.experimental.pallas import tpu as pltpu
from jax.sharding import PartitionSpec as P

HEADS = 12
HEAD_DIM = 64
ITEM_MOST = 256
EPS = 1e-12
SCALE = 0.125
MASKED = -1e30
FAR = 1e9
TILE = 128
PAIR = 2 * HEAD_DIM
WIDTHS = (256, 384, 640)
ROWS = 256
SMALL = 32
ORDER = (23, 1, 2, 1, 3, 2, 1, 3, 2, 1, 3, 2, 3, 1, 2, 3, 1, -1, 3, 2, 2, 3, -2, 3, 3, -3)
HALVES = 2
PARTS = 8
CHUNK = 512

bf16 = jnp.bfloat16
f32 = jnp.float32
i32 = jnp.int32
ANY = pl.BlockSpec(memory_space=pl.ANY)
HBM = pl.BlockSpec(memory_space=pltpu.HBM)
SMEM = pl.BlockSpec(memory_space=pltpu.SMEM)
VMEM = pl.BlockSpec(memory_space=pltpu.VMEM)


def params(mib, **kw):
    return pltpu.CompilerParams(vmem_limit_bytes=mib * 1024 * 1024, **kw)


def cost(flops, nbytes, trans=0):
    return pl.CostEstimate(flops=int(flops), bytes_accessed=int(nbytes), transcendentals=int(trans))


def mm(a, b):
    return lax.dot_general(a, b, (((1,), (0,)), ((), ())), preferred_element_type=f32)


def mm_nt(a, b):
    return lax.dot_general(a, b, (((1,), (1,)), ((), ())), preferred_element_type=f32)


def mm_tn(a, b):
    return lax.dot_general(a, b, (((0,), (0,)), ((), ())), preferred_element_type=f32)


def large(a):
    return a.size * a.dtype.itemsize > 512 * 1024


def call(kernel, out_shape, in_specs, out_specs, after=(), **kw):
    shapes = [
        pltpu.HBM(o.shape, o.dtype) if spec is HBM or large(o) else o for o, spec in zip(out_shape, out_specs)
    ]
    count = len(in_specs)

    def plain(*refs):
        return kernel(*refs[:count], *refs[count + len(after) :])

    specs = list(in_specs) + [ANY] * len(after)
    run = pl.pallas_call(plain, out_shape=shapes, in_specs=specs, out_specs=list(out_specs), **kw)

    def apply(*args):
        args = [
            pltpu.with_memory_space_constraint(a, pltpu.HBM) if spec is HBM or large(a) else a
            for a, spec in zip(args, in_specs)
        ]
        return run(*args, *after)

    return apply


def loads(pairs, sems):
    copies = [pltpu.make_async_copy(a, b, sems.at[i]) for i, (a, b) in enumerate(pairs)]
    for c in copies:
        c.start()
    return lambda i: copies[i].wait()


def out_copy(source, target, sem):
    c = pltpu.make_async_copy(source, target, sem)
    c.start()
    return c


def row_blocks(tokens):
    return [slice(r, r + ROWS) for r in range(0, tokens, ROWS)]


def front_kernel(
    place, lengths, bq, bv, x, wq, wk, wv, se, spans, q, k, v, xb, wb, ob, sems, osems
):
    ready = loads([(x, xb), (wq, wb.at[0]), (wk, wb.at[1]), (wv, wb.at[2])], sems)
    slots = lengths.shape[1]
    tokens = x.shape[0]
    ext = se.shape[1]
    reach = (ext - tokens) // 2
    step = max(d for d in range(8, 129, 8) if slots % d == 0)
    start = place[0] - reach
    pos = (lax.broadcasted_iota(i32, (1, ext), 1) + start).astype(f32)
    sizes = lengths[...].astype(f32)

    def scan(c, state):
        low, high = state
        index = lax.broadcasted_iota(i32, (step, slots), 0) + c * step
        upto = lax.broadcasted_iota(i32, (step, slots), 1) <= index
        ends = jnp.sum(jnp.where(upto, sizes, 0.0), axis=1, keepdims=True)
        before = ends <= pos
        low = jnp.maximum(low, jnp.max(jnp.where(before, ends, 0.0), axis=0, keepdims=True))
        high = jnp.minimum(high, jnp.min(jnp.where(before, FAR, ends), axis=0, keepdims=True))
        return low, high

    low, high = lax.fori_loop(
        0, slots // step, scan, (jnp.zeros((1, ext), f32), jnp.full((1, ext), FAR, f32))
    )
    real = (pos >= 0.0) & (high < FAR)
    local = lax.broadcasted_iota(i32, (1, ext), 1).astype(f32)
    offset = start.astype(f32)
    own = (local >= reach) & (local < reach + tokens)
    low_e = jnp.where(real, low - offset, local)
    high_e = jnp.where(real, high - offset, local + 1.0)
    shared = real & (
        ((local < reach) & (high_e > reach)) | ((local >= reach + tokens) & (low_e < reach + tokens))
    )
    used = own | shared
    low_e = jnp.where(used, low_e, 0.0)
    high_e = jnp.where(used, high_e, 0.0)
    se[0:1, :] = low_e
    se[1:2, :] = high_e
    spans[0] = jnp.sum(sizes).astype(i32)
    for t in range(ext // TILE):
        sl = slice(t * TILE, (t + 1) * TILE)
        some = high_e[:, sl] > low_e[:, sl]
        first = jnp.min(jnp.where(some, low_e[:, sl], FAR)).astype(i32)
        last = jnp.max(jnp.where(some, high_e[:, sl], -1.0)).astype(i32)
        at = first & ~15
        span = last - at
        kind = jnp.where(span <= WIDTHS[0], 1, jnp.where(span <= WIDTHS[1], 2, 3))
        wide = min(max(t * TILE - reach, 0), ext - WIDTHS[2])
        at = jnp.where(
            kind == 1,
            jnp.minimum(at, ext - WIDTHS[0]),
            jnp.where(kind == 2, jnp.minimum(at, ext - WIDTHS[1]), wide),
        )
        spans[8 + 2 * t] = jnp.where(last < 0, 0, kind)
        spans[9 + 2 * t] = at

    copies = []
    ready(0)
    for i, (b, out) in enumerate(((bq, q), (None, k), (bv, v))):
        ready(i + 1)
        for r in row_blocks(tokens):
            y = mm(xb[r, :], wb[i])
            if b is not None:
                y = y + b[...]
            y = y.astype(bf16)
            ob[i, r, :] = y * bf16(SCALE) if i == 0 else y
        copies.append(out_copy(ob.at[i], out, osems.at[i]))
    for c in copies:
        c.wait()


def front(place, lengths, x, wq, wk, wv, bq, bv, reach):
    tokens, width = x.shape
    ext = tokens + 2 * reach
    out = jax.ShapeDtypeStruct((tokens, width), bf16)
    return call(
        front_kernel,
        out_shape=(
            jax.ShapeDtypeStruct((8, ext), f32),
            jax.ShapeDtypeStruct((8 + 2 * (ext // TILE),), i32),
            out,
            out,
            out,
        ),
        in_specs=[SMEM, VMEM, VMEM, VMEM] + [HBM] * 4,
        out_specs=(VMEM, SMEM, HBM, HBM, HBM),
        scratch_shapes=[
            pltpu.VMEM((tokens, width), bf16),
            pltpu.VMEM((3, width, width), bf16),
            pltpu.VMEM((3, tokens, width), bf16),
            pltpu.SemaphoreType.DMA((4,)),
            pltpu.SemaphoreType.DMA((3,)),
        ],
        compiler_params=params(20),
        cost_estimate=cost(6 * tokens * width * width, 8 * tokens * width),
        name="front",
    )(place, lengths, bq, bv, x, wq, wk, wv)


def tile_bias(se, t, at, width):
    base = pl.multiple_of(t * TILE, TILE)
    low = se[0:1, pl.ds(base, TILE)]
    high = se[1:2, pl.ds(base, TILE)]
    key = (lax.broadcasted_iota(i32, (width, TILE), 0) + at).astype(f32)
    one = jnp.where((key >= low) & (key < high), 0.0, MASKED)
    some = jnp.where(high > low, 1.0, 0.0)
    return jnp.concatenate([one, one], axis=1), jnp.concatenate([some, some], axis=1)


def stacked(pair):
    lane = lax.broadcasted_iota(i32, pair.shape, 1)
    zero = jnp.zeros_like(pair)
    return jnp.concatenate(
        [jnp.where(lane < HEAD_DIM, pair, zero), jnp.where(lane < HEAD_DIM, zero, pair)], axis=0
    )


def unstacked(both):
    own = jnp.concatenate([both[:HEAD_DIM, :TILE], both[HEAD_DIM:, TILE:]], axis=0)
    return own.T


def each_tile(spans, first, last, tile):
    def each(t, _):
        kind, at = spans[8 + 2 * t], spans[9 + 2 * t]
        for i, span in enumerate(WIDTHS):
            pl.when(kind == i + 1)(functools.partial(tile, t, at, span))
        return 0

    lax.fori_loop(first, last, each, 0)


def attend_tile(se, q, kx, vx, attn, reach, t, at, span):
    width = q.shape[1]
    bias, _ = tile_bias(se, t, at, span)
    rows = pl.ds(pl.multiple_of(t * TILE - reach, TILE), TILE)
    window = pl.ds(pl.multiple_of(at, 16), span)
    pairs = [slice(p, p + PAIR) for p in range(0, width, PAIR)]
    scores = [mm_nt(kx[window, c], stacked(q[rows, c])) for c in pairs]
    soft = []
    for s in scores:
        s = s + bias
        weights = jnp.exp(s - jnp.max(s, axis=0, keepdims=True))
        soft.append((weights.astype(bf16), jnp.sum(weights, axis=0, keepdims=True)))
    for c, (weights, total) in zip(pairs, soft):
        attn[rows, c] = unstacked(mm_tn(vx[window, c], weights) / total).astype(bf16)


def attend_back_tile(se, qx, kx, vx, dox, dkx, dvx, t, at, span):
    width = qx.shape[1]
    bias, some = tile_bias(se, t, at, span)
    rows = pl.ds(pl.multiple_of(t * TILE, TILE), TILE)
    window = pl.ds(pl.multiple_of(at, 16), span)
    pairs = [slice(p, p + PAIR) for p in range(0, width, PAIR)]
    first = []
    for c in pairs:
        query, dout = stacked(qx[rows, c]), stacked(dox[rows, c])
        first.append((query, dout, mm_nt(kx[window, c], query), mm_nt(vx[window, c], dout)))
    second = []
    for query, dout, scores, dprob in first:
        scores = scores + bias
        weights = jnp.exp(scores - jnp.max(scores, axis=0, keepdims=True))
        probs = weights * (some / jnp.sum(weights, axis=0, keepdims=True))
        delta = jnp.sum(probs * dprob, axis=0, keepdims=True)
        second.append((probs.astype(bf16), (probs * (dprob - delta)).astype(bf16)))
    for c, (query, dout, _, _), (probs, dscore) in zip(pairs, first, second):
        dvx[window, c] += mm(probs, dout)
        dkx[window, c] += mm(dscore, query)
        qx[rows, c] = (unstacked(mm_tn(kx[window, c], dscore)) * SCALE).astype(bf16)


def attend_back_kernel(
    half, spans, se, bq, q, k, v, do, kh, vh, xl, xr, dl, dr, wq,
    dq, dk, dv, qx, kx, vx, dox, dkx, dvx, dkb, dvb, wb, xb, sems, osems,
):
    tokens = q.shape[0]
    reach = xl.shape[0]
    ext, some = kx.shape
    cols = pl.ds(half * some, some)
    own, low, high = pl.ds(reach, tokens), pl.ds(0, reach), pl.ds(reach + tokens, reach)
    ready = loads(
        [
            (wq.at[:, cols], wb),
            (xl, xb.at[low]),
            (xr, xb.at[pl.ds(reach, reach)]),
            (q.at[:, cols], qx.at[own]),
            (k.at[:, cols], kx.at[own]),
            (v.at[:, cols], vx.at[own]),
            (do.at[:, cols], dox.at[own]),
            (kh.at[pl.ds(0, reach), cols], kx.at[low]),
            (kh.at[pl.ds(reach, reach), cols], kx.at[high]),
            (vh.at[pl.ds(0, reach), cols], vx.at[low]),
            (vh.at[pl.ds(reach, reach), cols], vx.at[high]),
            (dl.at[:, cols], dox.at[low]),
            (dr.at[:, cols], dox.at[high]),
        ],
        sems,
    )
    dkx[...] = jnp.zeros_like(dkx)
    dvx[...] = jnp.zeros_like(dvx)
    for i in range(3):
        ready(i)
    bias = bq[...][half * some : (half + 1) * some]
    for at, to in ((0, 0), (reach, reach + tokens)):
        y = (mm(xb[at : at + reach, :], wb[...]) + bias).astype(bf16)
        qx[to : to + reach, :] = y * bf16(SCALE)
    for i in range(3, 13):
        ready(i)
    tile = functools.partial(attend_back_tile, se, qx, kx, vx, dox, dkx, dvx)
    each_tile(spans, 0, ext // TILE, tile)
    copies = [out_copy(qx.at[own], dq, osems.at[0])]
    dkb[...] = dkx[reach : reach + tokens, :].astype(bf16)
    copies.append(out_copy(dkb, dk, osems.at[1]))
    dvb[...] = dvx[reach : reach + tokens, :].astype(bf16)
    copies.append(out_copy(dvb, dv, osems.at[2]))
    for c in copies:
        c.wait()


def attend_back(half, halves, spans, se, q, k, v, do, kh, vh, xl, xr, dl, dr, wq, bq, after=()):
    tokens, width = q.shape
    reach = xl.shape[0]
    ext = tokens + 2 * reach
    some = width // halves
    out = jax.ShapeDtypeStruct((tokens, some), bf16)
    return call(
        functools.partial(attend_back_kernel, half),
        out_shape=(out, out, out),
        in_specs=[SMEM, VMEM, VMEM] + [HBM] * 11,
        out_specs=(HBM, HBM, HBM),
        scratch_shapes=[pltpu.VMEM((ext, some), bf16)] * 4
        + [pltpu.VMEM((ext, some), f32)] * 2
        + [pltpu.VMEM((tokens, some), bf16)] * 2
        + [pltpu.VMEM((width, some), bf16), pltpu.VMEM((2 * reach, width), bf16)]
        + [pltpu.SemaphoreType.DMA((13,)), pltpu.SemaphoreType.DMA((3,))],
        after=after,
        compiler_params=params(40),
        cost_estimate=cost(16e9 / halves, 20 * tokens * some),
        name="attend_back_%d" % half,
    )(spans, se, bq, q, k, v, do, kh, vh, xl, xr, dl, dr, wq)


LAYERS = [4]


def write_group(block, send, keep, buf, sems, place):
    here, layer = place[1], place[2]
    slots, rows = buf.shape[:2]
    half = rows // 2
    layers = LAYERS[0]
    chunk = half // layers

    def copies(slot, x, y, out):
        return (
            pltpu.make_async_copy(
                buf.at[slot, pl.ds(0, half)],
                out.at[pl.ds(pl.multiple_of((2 * x + y) * half, half), half)],
                sems.at[slot, 0],
            ),
            pltpu.make_async_copy(
                buf.at[slot, pl.ds(half, half)],
                out.at[pl.ds(pl.multiple_of((4 + 2 * y + x) * half, half), half)],
                sems.at[slot, 1],
            ),
        )

    def free(slot):
        for c in copies(slot, 0, 0, keep):
            c.wait()

    for part in range(PARTS):
        to = part ^ here
        core, x, y = to & 1, (to >> 1) & 1, (to >> 2) & 1
        slot = part % slots
        value = block(part).astype(bf16)
        if part >= slots:
            free(slot)
        for z in range(layers):
            at = (z ^ layer) * chunk
            for h in (0, half):
                buf[slot, pl.ds(pl.multiple_of(h + at, chunk), chunk), :] = value[h + z * chunk : h + (z + 1) * chunk]

        def start(out, slot=slot, x=x, y=y):
            for c in copies(slot, x, y, out):
                c.start()

        pl.when(core == 1)(functools.partial(start, send))
        pl.when(core == 0)(functools.partial(start, keep))
    for slot in range(slots):
        free(slot)


def group_shapes(rows, width):
    return (jax.ShapeDtypeStruct((rows // 2, width), bf16),) * 2


def group_scratch(rows, width):
    return [pltpu.VMEM((2, rows // PARTS, width), bf16), pltpu.SemaphoreType.DMA((2, 2))]


def gelu_both(z):
    u = jnp.abs(z) * 0.7071067811865476
    t = 1.0 / (1.0 + 0.3275911 * u)
    bell = jnp.exp(-0.5 * z * z)
    poly = t * (
        0.5 * 0.254829592
        + t * (0.5 * -0.284496736 + t * (0.5 * 1.421413741 + t * (0.5 * -1.453152027 + t * (0.5 * 1.061405429))))
    )
    tail = poly * bell
    cdf = jnp.where(z >= 0.0, 1.0 - tail, tail)
    return z * cdf, cdf + z * bell * 0.3989422804014327


def center(v):
    mean = jnp.mean(v, axis=1, keepdims=True)
    c = v - mean
    rstd = lax.rsqrt(jnp.mean(c * c, axis=1, keepdims=True) + EPS)
    return c * rstd, rstd


def center_back(e, xhat, rstd):
    return rstd * (
        e - jnp.mean(e, axis=1, keepdims=True) - xhat * jnp.mean(e * xhat, axis=1, keepdims=True)
    )


def colsum(v):
    return jnp.sum(v, axis=0, keepdims=True)


def layer_kernel(
    place, spans, se, bv, bo, g1, s1, bu, bd, g2, s2, q, k, v, xl, xr, x, dy, wk, wv, wo, wu, wd,
    rstd1, vec, attn, kh, vh, out, slope, mid_low, xhat1, d_two, d_down, send, keep,
    qb, kx, vx, xlb, xrb, wkb, wvb, khb, vhb, attb, xb, dyb, wob, wub, wdb, act, slb, xhb, lowb, two, ob, ddb, buf, sems, osems, gsems,
):
    tokens, width = x.shape
    ff = wu.shape[1]
    reach = xl.shape[0]
    ready = loads(
        [
            (wk, wkb), (xl, xlb), (xr, xrb), (wv, wvb),
            (k, kx.at[pl.ds(reach, tokens)]), (v, vx.at[pl.ds(reach, tokens)]), (q, qb),
            (wo, wob), (x, xb), (wu, wub), (wd, wdb), (dy, dyb),
        ],
        sems,
    )
    copies = []

    def put(source, target):
        copies.append(out_copy(source, target, osems.at[len(copies)]))

    for i in range(3):
        ready(i)
    for part, at, to in ((xlb, 0, 0), (xrb, reach, reach + tokens)):
        y = mm(part[...], wkb[...]).astype(bf16)
        kx[to : to + reach, :] = y
        khb[at : at + reach, :] = y
    ready(3)
    for part, at, to in ((xlb, 0, 0), (xrb, reach, reach + tokens)):
        y = (mm(part[...], wvb[...]) + bv[...]).astype(bf16)
        vx[to : to + reach, :] = y
        vhb[at : at + reach, :] = y
    put(khb, kh)
    put(vhb, vh)
    for i in (4, 5, 6):
        ready(i)
    tile = functools.partial(attend_tile, se, qb, kx, vx, attb, reach)
    each_tile(spans, reach // TILE, (reach + tokens) // TILE, tile)
    put(attb, attn)

    ready(7)
    ready(8)
    blocks = row_blocks(tokens)
    branch = [mm(attb[r, :], wob[...]) for r in blocks]
    for r, b in zip(blocks, branch):
        xh1, r1 = center(xb[r, :].astype(f32) + b + bo[...])
        mid = xh1 * g1[...] + s1[...]
        xhb[r, :] = xh1
        rstd1[r, :] = jnp.broadcast_to(r1, (ROWS, rstd1.shape[1]))
        lowb[r, :] = mid.astype(bf16)
        two[r, :] = mid + bd[...]
    put(xhb, xhat1)
    put(lowb, mid_low)

    ready(9)
    ready(10)

    def ups(c):
        return [mm(lowb[r, :], wub[:, c : c + CHUNK]) for r in blocks]

    up = ups(0)
    for c in range(0, ff, CHUNK):
        cols = slice(c, c + CHUNK)
        now = up
        if c + CHUNK < ff:
            up = ups(c + CHUNK)
        for r, z in zip(blocks, now):
            a, s = gelu_both(z + bu[...][cols])
            act[r, cols] = a.astype(bf16)
            slb[r, cols] = s.astype(bf16)
        for r in blocks:
            two[r, :] += mm(act[r, cols], wdb[cols, :])
        put(slb.at[:, pl.ds(c, CHUNK)], slope.at[:, pl.ds(c, CHUNK)])

    ready(11)
    sums = [0.0, 0.0, 0.0]
    for r in blocks:
        xh2, r2 = center(two[r, :])
        token = place[0] + r.start + lax.broadcasted_iota(i32, (ROWS, 1), 0)
        valid = jnp.where(token < spans[0], 1.0, 0.0)
        ob[r, :] = ((xh2 * g2[...] + s2[...]) * valid).astype(bf16)
        d = dyb[r, :].astype(f32) * valid
        d2 = center_back(d * g2[...], xh2, r2)
        two[r, :] = d2
        d2 = d2.astype(bf16)
        ddb[r, :] = d2
        for i, term in enumerate((d2.astype(f32), d * xh2, d)):
            sums[i] = sums[i] + colsum(term)
    put(ddb, d_down)
    put(two, d_two)
    put(ob, out)
    vec[3:8, :] = jnp.zeros((5, width), f32)
    for i in range(3):
        vec[i : i + 1, :] = sums[i]

    size = ff // PARTS
    write_group(lambda p: mm_tn(act[:, p * size : (p + 1) * size], ddb[...]), send, keep, buf, gsems, place)
    for c in copies:
        c.wait()


def layer(place, spans, se, q, k, v, xl, xr, x, dy, wk, wv, wo, wu, wd, bv, bo, g1, s1, bu, bd, g2, s2):
    tokens, width = x.shape
    ff = wu.shape[1]
    reach = xl.shape[0]
    ext = tokens + 2 * reach
    shape = lambda n, t, rows=tokens: jax.ShapeDtypeStruct((rows, n), t)
    vm = lambda rows, n, t: pltpu.VMEM((rows, n), t)
    return call(
        layer_kernel,
        out_shape=(
            shape(128, f32),
            shape(width, f32, 8),
            shape(width, bf16),
            shape(width, bf16, 2 * reach),
            shape(width, bf16, 2 * reach),
            shape(width, bf16),
            shape(ff, bf16),
            shape(width, bf16),
            shape(width, f32),
            shape(width, f32),
            shape(width, bf16),
        )
        + group_shapes(ff, width),
        in_specs=[SMEM, SMEM] + [VMEM] * 9 + [HBM] * 12,
        out_specs=(VMEM, VMEM) + (HBM,) * 11,
        scratch_shapes=[
            vm(tokens, width, bf16),
            vm(ext, width, bf16),
            vm(ext, width, bf16),
            vm(reach, width, bf16),
            vm(reach, width, bf16),
            vm(width, width, bf16),
            vm(width, width, bf16),
            vm(2 * reach, width, bf16),
            vm(2 * reach, width, bf16),
            vm(tokens, width, bf16),
            vm(tokens, width, bf16),
            vm(tokens, width, bf16),
            vm(width, width, bf16),
            vm(width, ff, bf16),
            vm(ff, width, bf16),
            vm(tokens, ff, bf16),
            vm(tokens, ff, bf16),
            vm(tokens, width, f32),
            vm(tokens, width, bf16),
            vm(tokens, width, f32),
            vm(tokens, width, bf16),
            vm(tokens, width, bf16),
        ]
        + group_scratch(ff, width)[:1]
        + [pltpu.SemaphoreType.DMA((12,)), pltpu.SemaphoreType.DMA((8 + ff // CHUNK,))]
        + group_scratch(ff, width)[1:],
        compiler_params=params(56),
        cost_estimate=cost(2 * tokens * width * (width + 3 * ff) + 8e9, 40 * tokens * width, 2 * tokens * ff),
        name="layer",
    )(place, spans, se, bv, bo, g1, s1, bu, bd, g2, s2, q, k, v, xl, xr, x, dy, wk, wv, wo, wu, wd)


def back_kernel(
    g1, rstd1, dd, slope, wd, wu, d_two, xhat1, wo,
    d_up, vec, bup, d_one, d_branch, d_attn, dmid, d2b, xhb, wob, oneb, brb, atb, sems, osems,
):
    c = pl.program_id(0)
    tokens, width = dd.shape
    pairs = [(d_two, d2b), (xhat1, xhb), (wo, wob)]
    arriving = [pltpu.make_async_copy(a, b, sems.at[i]) for i, (a, b) in enumerate(pairs)]

    @pl.when(c == 0)
    def _():
        for a in arriving:
            a.start()
        dmid[...] = jnp.zeros_like(dmid)
        vec[...] = jnp.zeros_like(vec)

    blocks = row_blocks(tokens)
    d_act = [mm_nt(dd[r, :], wd[...]) for r in blocks]
    total = 0.0
    for r, d in zip(blocks, d_act):
        du = (slope[r, :].astype(f32) * d).astype(bf16)
        d_up[r, :] = du
        total = total + colsum(du.astype(f32))
    bup[pl.ds(c, 1), :] = total

    for r in blocks:
        dmid[r, :] += mm_nt(d_up[r, :], wu[...])

    @pl.when(c == pl.num_programs(0) - 1)
    def _():
        for a in arriving:
            a.wait()
        sums = [0.0, 0.0, 0.0]
        copies = []
        for i, r in enumerate(blocks):
            d_mid = dmid[r, :] + d2b[r, :]
            xh = xhb[r, :]
            d1 = center_back(d_mid * g1[...], xh, rstd1[r, 0:1])
            oneb[r, :] = d1
            d1 = d1.astype(bf16)
            brb[r, :] = d1
            for n, term in enumerate((d_mid * xh, d_mid, d1.astype(f32))):
                sums[n] = sums[n] + colsum(term)
        for i, r in enumerate(blocks):
            atb[r, :] = mm_nt(brb[r, :], wob[...]).astype(bf16)
            at = pl.ds(r.start, ROWS)
            for n, (a, b) in enumerate(((oneb, d_one), (brb, d_branch), (atb, d_attn))):
                copies.append(out_copy(a.at[at], b.at[at], osems.at[3 * i + n]))
        for n in range(3):
            vec[n : n + 1, :] = sums[n]
        for a in copies:
            a.wait()


def back(d_two, d_down, slope, xhat1, rstd1, wd, wu, wo, g1, after=()):
    tokens, width = d_two.shape
    ff = wu.shape[1]
    full = lambda a: pl.BlockSpec(a.shape, lambda c: (0,) * a.ndim)
    col = lambda rows: pl.BlockSpec((rows, CHUNK), lambda c: (0, c))
    shape = lambda n, t: jax.ShapeDtypeStruct((tokens, n), t)
    vec = jax.ShapeDtypeStruct((8, width), f32)
    bup = jax.ShapeDtypeStruct((ff // CHUNK, CHUNK), f32)
    return call(
        back_kernel,
        grid=(ff // CHUNK,),
        out_shape=(shape(ff, bf16), vec, bup, shape(width, f32), shape(width, bf16), shape(width, bf16)),
        in_specs=[full(g1), full(rstd1), full(d_down), col(tokens), pl.BlockSpec((CHUNK, width), lambda c: (c, 0)), col(width)]
        + [HBM] * 3,
        out_specs=(col(tokens), full(vec), full(bup), HBM, HBM, HBM),
        scratch_shapes=[
            pltpu.VMEM((tokens, width), f32),
            pltpu.VMEM((tokens, width), f32),
            pltpu.VMEM((tokens, width), f32),
            pltpu.VMEM((width, width), bf16),
            pltpu.VMEM((tokens, width), f32),
            pltpu.VMEM((tokens, width), bf16),
            pltpu.VMEM((tokens, width), bf16),
            pltpu.SemaphoreType.DMA((3,)),
            pltpu.SemaphoreType.DMA((3 * (tokens // ROWS),)),
        ],
        after=after,
        compiler_params=params(34, dimension_semantics=("arbitrary",)),
        cost_estimate=cost(2 * tokens * width * (width + 2 * ff), 30 * tokens * width),
        name="back",
    )(g1, rstd1, d_down, slope, wd, wu, d_two, xhat1, wo)


def up_grad_kernel(place, mid_low, d_up, send, keep, lowb, upb, buf, gsems, sems):
    width = mid_low.shape[1]
    size = width // 2
    many = d_up.shape[1] // width
    ready = loads(
        [(mid_low, lowb)] + [(d_up.at[:, pl.ds(n * width, width)], upb.at[n]) for n in range(many)], sems
    )
    ready(0)

    def block(part):
        if part % 2 == 0:
            ready(1 + part // 2)
        rows = (part % 2) * size
        return mm_tn(lowb[:, rows : rows + size], upb[part // 2])

    write_group(block, send, keep, buf, gsems, place)


def up_grad(place, mid_low, d_up, after=()):
    tokens, width = mid_low.shape
    ff = d_up.shape[1]
    return call(
        up_grad_kernel,
        out_shape=group_shapes(ff, width),
        in_specs=[SMEM, HBM, HBM],
        out_specs=(HBM, HBM),
        scratch_shapes=[pltpu.VMEM((tokens, width), bf16), pltpu.VMEM((ff // width, tokens, width), bf16)]
        + group_scratch(ff, width)
        + [pltpu.SemaphoreType.DMA((1 + ff // width,))],
        after=after,
        compiler_params=params(20),
        cost_estimate=cost(2 * tokens * width * ff, 14 * tokens * width),
        name="up_grad",
    )(place, mid_low, d_up)


def rest_grad_kernel(halves, place, vec_a, vec_b, bup, attn, x, d_branch, *refs):
    parts, (send, keep, lhs, rhs, buf, small, gsems, sems, ssems) = refs[: 3 * halves], refs[3 * halves :]
    tokens, width = x.shape
    size = width // 2
    some = width // halves
    pairs = [(attn, lhs.at[0]), (d_branch, rhs.at[0]), (x, lhs.at[1])]
    for n in range(3):
        for h in range(halves):
            pairs.append((parts[3 * h + n], rhs.at[n + 1, :, pl.ds(h * some, some)]))
    ready = loads(pairs, sems)
    ready(0)
    ready(1)

    def block(part):
        which = part // 2
        if part == 2:
            ready(2)
        if which > 0 and part % 2 == 0:
            for h in range(halves):
                ready(3 + (which - 1) * halves + h)
        rows = (part % 2) * size
        return mm_tn(lhs[min(which, 1), :, rows : rows + size], rhs[which])

    write_group(block, send, keep, buf, gsems, place)
    ones = jnp.ones((8, tokens), bf16)
    row = lax.broadcasted_iota(i32, (8, width), 0)
    sums = jnp.where(row == 0, mm(ones, rhs[1]), jnp.where(row == 1, mm(ones, rhs[3]), 0.0))
    lines = [vec_a[...], sums, vec_b[...], bup[...]]
    have = sum(v.shape[0] for v in lines)
    lines.append(jnp.zeros((SMALL - have, width), f32))
    small[...] = jnp.concatenate(lines, axis=0).astype(bf16)
    end = pl.ds(2 * width, SMALL)
    copies = [out_copy(small, o.at[end], ssems.at[i]) for i, o in enumerate((send, keep))]
    for c in copies:
        c.wait()


def rest_grad(place, attn, x, d_branch, parts, vecs, after=()):
    tokens, width = x.shape
    rows = 4 * width
    halves = len(parts)
    out = jax.ShapeDtypeStruct((rows // 2 + SMALL, width), bf16)
    return call(
        functools.partial(rest_grad_kernel, halves),
        out_shape=(out, out),
        in_specs=[SMEM, VMEM, VMEM, VMEM] + [HBM] * (3 + 3 * halves),
        out_specs=(HBM, HBM),
        scratch_shapes=[pltpu.VMEM((2, tokens, width), bf16), pltpu.VMEM((4, tokens, width), bf16)]
        + group_scratch(rows, width)[:1]
        + [pltpu.VMEM((SMALL, width), bf16)]
        + group_scratch(rows, width)[1:]
        + [pltpu.SemaphoreType.DMA((3 + 3 * halves,)), pltpu.SemaphoreType.DMA((2,))],
        after=after,
        compiler_params=params(20),
        cost_estimate=cost(8 * tokens * width * width, 20 * tokens * width),
        name="rest_grad",
    )(place, *vecs, attn, x, d_branch, *sum(map(tuple, parts), ()))


def inputs_grad_kernel(halves, d_one, *refs):
    parts, (wq, wk, wv, out) = refs[: 3 * halves], refs[3 * halves :]
    total = d_one[...]
    some = wq.shape[1] // halves
    for h in range(halves):
        for g, w in zip(parts[3 * h : 3 * h + 3], (wq, wk, wv)):
            total = total + mm_nt(g[...], w[:, h * some : (h + 1) * some])
    out[...] = total


def inputs_grad(d_one, parts, wq, wk, wv, after=()):
    tokens, width = d_one.shape
    halves = len(parts)
    tok = lambda n: pl.BlockSpec((ROWS, n), lambda i: (i, 0))
    full = pl.BlockSpec((width, width), lambda i: (0, 0))
    return call(
        functools.partial(inputs_grad_kernel, halves),
        grid=(tokens // ROWS,),
        out_shape=(jax.ShapeDtypeStruct((tokens, width), f32),),
        in_specs=[tok(width)] + [tok(width // halves)] * (3 * halves) + [full] * 3,
        out_specs=(tok(width),),
        after=after,
        compiler_params=params(16, dimension_semantics=("arbitrary",)),
        cost_estimate=cost(6 * tokens * width * width, 20 * tokens * width),
        name="inputs_grad",
    )(d_one, *sum(map(tuple, parts), ()), wq, wk, wv)


def swap(value, axis, bit):
    count = lax.axis_size(axis)
    return lax.ppermute(value, axis, [(i, i ^ bit) for i in range(count)])


def plus(a, b):
    return (a.astype(f32) + b.astype(f32)).astype(bf16)


def layer_bits():
    return list(range(1, lax.axis_size("dp")))


def far_bits():
    bit, bits = PARTS, []
    while bit < lax.axis_size("seq"):
        bits.append(bit)
        bit *= 2
    return bits


def axis_bits(axis):
    return [1 << n for n in range((lax.axis_size(axis) - 1).bit_length())]


class Sum:
    def __init__(self, send, keep, tail=0):
        self.mine, self.got, self.payload, self.tail = [keep], [], [send], tail
        self.swaps = [("seq", 1)]
        self.steps = self.run()

    def receive(self, token):
        if self.got:
            *self.got, _ = lax.optimization_barrier((*self.got, token))
            next(self.steps)

    def send(self):
        self.got = [swap(p, *s) for p, s in zip(self.payload, self.swaps)]

    def tailed(self, payloads):
        rows = [p.reshape(-1, p.shape[-1]) for p in payloads]
        if self.tail:
            rows[0] = jnp.concatenate([rows[0], self.small], axis=0)
        return rows

    def untailed(self, like):
        if self.tail:
            self.small = plus(self.small, self.got[0][-self.tail :])
            self.got[0] = self.got[0][: -self.tail]
        return [g.reshape(m.shape) for g, m in zip(self.got, like)]

    def run(self):
        keep, got = self.mine[0], self.got[0]
        width = keep.shape[-1]
        both = plus(keep, got)
        if self.tail:
            self.small, both = both[-self.tail :], both[: -self.tail]
        layers = axis_bits("dp")
        both = both.reshape((2, 2, 2) + (2,) * len(layers) + (-1, width))
        parts = [both[0], both[1]]
        for bits in ((2, 4), (4, 2)):
            keeps = [p[0] for p in parts]
            self.payload, self.swaps = self.tailed([p[1] for p in parts]), [("seq", b) for b in bits]
            yield
            parts = list(map(plus, keeps, self.untailed(keeps)))
        part = jnp.stack(parts, axis=-3)
        for bit in layers:
            axis = part.ndim - 4
            keep = lax.index_in_dim(part, 0, axis, keepdims=False)
            self.payload, self.swaps = self.tailed([lax.index_in_dim(part, 1, axis, keepdims=False)]), [("dp", bit)]
            yield
            part = plus(keep, self.untailed([keep])[0])
        for bit in far_bits():
            part = plus(part, swap(part, "seq", bit))
            if self.tail:
                self.small = plus(self.small, swap(self.small, "seq", bit))
        for bit in reversed(layers):
            self.payload, self.swaps = [part], [("dp", bit)]
            yield
            part = jnp.stack([part, self.got[0]], axis=part.ndim - 3)
        parts = [lax.index_in_dim(part, n, part.ndim - 3, keepdims=False) for n in range(2)]
        for bits in ((4, 2), (2, 4)):
            self.payload, self.swaps = parts, [("seq", b) for b in bits]
            yield
            parts = [jnp.stack(pair) for pair in zip(parts, self.got)]
        whole = jnp.stack(parts).reshape(8, -1, width)
        self.payload, self.swaps = [whole], [("seq", 1)]
        yield
        self.result = (whole, self.got[0])
        self.payload = []
        yield


def advance(token, *sums):
    for s in sums:
        s.receive(token)
    payloads = lax.optimization_barrier(tuple(p for s in sums for p in s.payload))
    at = 0
    for s in sums:
        s.payload = list(payloads[at : at + len(s.payload)])
        at += len(s.payload)
        s.send()
    return payloads[0] if payloads else token


def spread_kernel(kind, place, ma, mb, oa, ob, *refs):
    outs, (buf, sems) = refs[:-2], refs[-2:]
    j = pl.program_id(0)
    here, layer = place[1], place[2]
    half = ma.shape[1]
    size = 2 * half
    layers = LAYERS[0]
    chunk = half // layers
    width = ma.shape[2]

    def copies(step):
        part = step ^ here
        slot = step & 1
        src = buf.at[slot]
        if kind == "down":
            return [(None, pltpu.make_async_copy(src, outs[0].at[pl.ds(pl.multiple_of(part * size, size), size)], sems.at[slot]))]
        at = pl.ds(pl.multiple_of((part & 1) * size, size), size)
        which = part >> 1
        if kind == "up":
            cols = pl.ds(pl.multiple_of(which * width, width), width)
            return [(None, pltpu.make_async_copy(src, outs[0].at[at, cols], sems.at[slot]))]
        return [(which == n, pltpu.make_async_copy(src, o.at[at], sems.at[slot])) for n, o in enumerate(outs)]

    def start(step):
        for cond, c in copies(step):
            if cond is None:
                c.start()
            else:
                pl.when(cond)(c.start)

    def wait(step):
        copies(step)[0][1].wait()

    pl.when(j >= 2)(lambda: wait(j - 2))
    slot = j & 1

    def fill(a, b):
        for z in range(layers):
            to = (z ^ layer) * chunk
            rows = slice(z * chunk, (z + 1) * chunk)
            buf[slot, pl.ds(pl.multiple_of(to, chunk), chunk), :] = a[0, rows, :].astype(f32)
            buf[slot, pl.ds(pl.multiple_of(half + to, chunk), chunk), :] = b[0, rows, :].astype(f32)

    pl.when((j & 1) == 0)(lambda: fill(ma, mb))
    pl.when((j & 1) == 1)(lambda: fill(oa, ob))
    start(j)

    @pl.when(j == PARTS - 1)
    def _():
        wait(j - 1)
        wait(j)


def spread(kind, place, mine, other, after=()):
    half, width = mine.shape[1:]
    rows = 2 * half * PARTS
    a = pl.BlockSpec((1, half, width), lambda j: (2 * ((j >> 1) & 1) + (j >> 2), 0, 0))
    b = pl.BlockSpec((1, half, width), lambda j: (4 + 2 * (j >> 2) + ((j >> 1) & 1), 0, 0))
    if kind == "down":
        shapes = [(rows, width)]
    elif kind == "up":
        shapes = [(width, rows)]
    else:
        shapes = [(width, width)] * 4
    return call(
        functools.partial(spread_kernel, kind),
        grid=(PARTS,),
        out_shape=[jax.ShapeDtypeStruct(s, f32) for s in shapes],
        in_specs=[SMEM, a, b, a, b],
        out_specs=[HBM] * len(shapes),
        after=after,
        scratch_shapes=[pltpu.VMEM((2, 2 * half, width), f32), pltpu.SemaphoreType.DMA((2,))],
        compiler_params=params(12, dimension_semantics=("arbitrary",)),
        cost_estimate=cost(rows * width, 6 * rows * width),
        name="spread_" + kind,
    )(place, mine, mine, other, other)


def sum_small(vec):
    for axis in ("seq", "dp"):
        bit = 1
        while bit < lax.axis_size(axis):
            vec = vec + swap(vec, axis, bit)
            bit *= 2
    return vec


def neighbours(value, reach):
    count = lax.axis_size("seq")
    up = [(i, i + 1) for i in range(count - 1)]
    low = lax.ppermute(value[-reach:], "seq", up)
    high = lax.ppermute(value[:reach], "seq", [(b, a) for a, b in up])
    return low, high


def body(
    inputs, lengths, w_query, b_query, w_key, w_value, b_value, w_out, b_out, gain_one, shift_one,
    w_up, b_up, w_down, b_down, gain_two, shift_two, d_output,
):
    rows, tokens, width = inputs.shape
    reach = ITEM_MOST
    LAYERS[0] = lax.axis_size("dp")
    here = lax.axis_index("seq")
    place = jnp.stack([here * tokens, here & (PARTS - 1), lax.axis_index("dp")]).astype(i32)
    x = inputs.reshape(tokens, width)
    dy = d_output.reshape(tokens, width)

    xl, xr = neighbours(x, reach)
    se, spans, q, k, v = front(place, lengths, x, w_query, w_key, w_value, b_query, b_value, reach)
    rstd1, vec_a, attn, kh, vh, output, slope, mid_low, xhat1, d_two, d_down, send1, keep1 = layer(
        place, spans, se, q, k, v, xl, xr, x, dy, w_key, w_value, w_out, w_up, w_down,
        b_value, b_out, gain_one, shift_one, b_up, b_down, gain_two, shift_two,
    )
    one = Sum(send1, keep1)
    token = advance(d_two, one)
    d_up, vec_b, bup, d_one, d_branch, d_attn = back(
        d_two, d_down, slope, xhat1, rstd1, w_down, w_up, w_out, gain_one, after=[token]
    )
    token = advance(d_attn, one)
    dl, dr = neighbours(d_attn, reach)
    send2, keep2 = up_grad(place, mid_low, d_up, after=[token])
    two = Sum(send2, keep2)
    token = advance(send2, two)
    args = (HALVES, spans, se, q, k, v, d_attn, kh, vh, xl, xr, dl, dr, w_query, b_query)
    parts = [attend_back(0, *args, after=[token])]
    token = advance(parts[0][0], one, two)
    parts.append(attend_back(1, *args, after=[token]))
    token = advance(parts[1][0], one)
    send3, keep3 = rest_grad(place, attn, x, d_branch, parts, [vec_a, vec_b, bup.reshape(-1, width)], after=[token])
    three = Sum(send3, keep3, SMALL)
    token = advance(send3, one, two, three)
    (d_inputs,) = inputs_grad(d_one, parts, w_query, w_key, w_value, after=[token])
    token = d_inputs
    sums = {1: one, 2: two, 3: three}
    for event in ORDER:
        if event < 0:
            kind = ("down", "up", "rest")[-event - 1]
            grads = spread(kind, place, *sums[-event].result, after=[token])
            token = grads[0]
            if kind == "down":
                (g_w_down,) = grads
            elif kind == "up":
                (g_w_up,) = grads
            else:
                g_w_out, g_w_query, g_w_key, g_w_value = grads
        else:
            token = advance(token, *[sums[int(g)] for g in str(event)])
    small = three.small.astype(f32)
    ff = w_up.shape[1]
    many = ff // width
    return (
        output.reshape(rows, tokens, width),
        d_inputs.reshape(rows, tokens, width),
        g_w_query,
        small[8],
        g_w_key,
        g_w_value,
        small[9],
        g_w_out,
        small[18],
        small[16],
        small[17],
        g_w_up,
        small[24 : 24 + many].reshape(ff),
        g_w_down,
        small[0],
        small[1],
        small[2],
    )


def solution(mesh):
    split, whole = P("dp", "seq", None), P()
    return jax.shard_map(
        body,
        mesh=mesh,
        in_specs=(split, P("dp", None)) + (whole,) * 15 + (split,),
        out_specs=(split, split) + (whole,) * 15,
        check_vma=False,
    )
```

time: 422 us -> 304 us (0.72)
  starting transfers between devices: 111 us -> 65.6 us
  waiting for transfers between devices: 105 us -> 62.3 us
  Pallas kernels: 176 us -> 142 us
  local copies, waits for them, and re-layouts: 10.9 us -> 17.9 us
    ppermute x53 -> x42, starting transfers between devices: 101 us -> 57.5 us  [swap(): return lax.ppermute(value, axis, [(i, i ^ bit) for i in range(count)])]
    ppermute x53 -> x42, waiting for transfers between devices: 105 us -> 62.3 us  [swap(): return lax.ppermute(value, axis, [(i, i ^ bit) for i in range(count)])]
    pallas_call x11, Pallas kernels: 176 us -> 142 us  [apply(): return run(*args, *after)]
    unnamed x38 -> x55, local copies, waits for them, and re-layouts: 1.81 us -> 13.2 us
    reshape x9 -> x2, local copies, waits for them, and re-layouts: 5.25 us -> 0.77 us  [the longest x1 0.76 us: body(): small[24:24 + many].reshape(ff)]
  transfers between devices with their start and end apart: 57 -> 46, of which waited for: 22 -> 23; matrix products, arithmetic and copies ran while one was open for 4% -> 2% of each run, Pallas kernels for 23% -> 29%
where the time goes in v2:
time: 304 us; the launch traced here: 298 us
  Pallas kernels  142 us (47%)
  starting transfers between devices  65.6 us (22%)
  waiting for transfers between devices  62.3 us (20%)
  local copies, waits for them, and re-layouts  17.9 us (6%)
  other arithmetic  8.24 us (3%)
    pallas_call x11, Pallas kernels, apply(): return run(*args, *after)  142 us
    ppermute x42, waiting for transfers between devices, swap(): return lax.ppermute(value, axis, [(i, i ^ bit) for i in range(count)])  62.3 us
    ppermute x42, starting transfers between devices, swap(): return lax.ppermute(value, axis, [(i, i ^ bit) for i in range(count)])  57.5 us
    unnamed x55, local copies, waits for them, and re-layouts  13.2 us
  transfers between devices with their start and end apart: 46, of which 23 were waited for; matrix products, arithmetic and copies ran while one was open for 2% of the time, Pallas kernels for 29%

profile of v2, /device:TPU:0, one launch (start us, length us, event | category | flops | bytes accessed | tf_op | source)
XLA Modules:
  0.0 297.8 jit_solution(12284740675034684020)
XLA Ops:
  5.7 7.5 %front.1 = (f32[8,1280]{1,0:T(8,128)S(1)}, s32[28]{0:T(128)S(1)}, bf16[768,768]{1,0:T(8,128)(2,1)}, bf16[768,768]{1,0:T(8,128)(2,1)}, bf16[768,768]{1,0:T(8,128)(2,1)}) custom-call(s32[3]{0:T(128)S(1)} %pad_add_fusion.refs_0_, s32[1,784]{1,0:T(1,128)S(1)} %copy-done.7, f32[768]{0:T(1024)S(1)} %copy-done.6, f32[768]{0:T(1024)S(1)} %copy-done.4, ...), custom_call_target="tpu_custom_call" | custom-call | flops 2717908992 | bytes 4718592 | tf_op jit(solution)/shard_map/front/pallas_call | solution.py:77
  14.7 35.4 %layer.1 = (f32[768,128]{1,0:T(8,128)}, f32[8,768]{1,0:T(8,128)}, bf16[768,768]{1,0:T(8,128)(2,1)}, bf16[512,768]{1,0:T(8,128)(2,1)}, bf16[512,768]{1,0:T(8,128)...) custom-call(s32[3]{0:T(128)} %copy-done, ...), custom_call_target="tpu_custom_call" | custom-call | flops 19777605632 | bytes 23592960 | tf_op jit(solution)/shard_map/layer/pallas_call | solution.py:77
  50.2 3.5 %collective-permute-start.4 = (bf16[1536,768]{1,0:T(8,128)(2,1)}, bf16[1536,768]{1,0:T(8,128)(2,1)S(1)}, u32[]{:S(2)}, u32[]{:S(2)}) collective-permute-start(bf16[1536,768]{1,0:T(8,128)(2,1)} %get-tuple-element.135.refs_9_), channel_id=1, source_target_pairs={{0,1},{1,0},{2,3},{3,2},{4,5},{5,4},{6,7},{7,6},{8,9},{9,8},{10,11... | collective-permute-start | bytes 7077896 | tf_op jit(solution)/shard_map/ppermute | solution.py:802
  56.3 17.4 %back.1 = (bf16[768,3072]{1,0:T(8,128)(2,1)}, f32[8,768]{1,0:T(8,128)S(1)}, f32[6,512]{1,0:T(8,128)S(1)}, f32[768,768]{1,0:T(8,128)}, bf16[768,768]{1,0:T(8,128)(2,1)}, /*index=5*/bf16[768,768]{1,0:T(8,128)(2,1)}) custom-call(f32[768]{0:T(1024)S(1)} %copy-done.5, f32[768,128]{1,0:T(8,128)S(1)} %copy-done.8, bf16[768,768]{1,0:T(8,128)(2,1)} %get-tuple-element.131.refs_2_, ...), custom_call_target="tpu_custom_call" | custom-call | flops 8153726976 | bytes 17694720 | tf_op jit(solution)/shard_map/back/pallas_call | solution.py:77
  75.3 9.3 %up_grad.1 = (bf16[1536,768]{1,0:T(8,128)(2,1)}, bf16[1536,768]{1,0:T(8,128)(2,1)}) custom-call(s32[3]{0:T(128)S(1)} %copy-done.1, bf16[768,768]{1,0:T(8,128)(2,1)} %get-tuple-element.140.refs_1_, bf16[768,3072]{1,0:T(8,128)(2,1)} %get-tuple-element.141.refs_2_, bf16[384,768]{1,0:T(8,128)(2,1)S(1)} %get-tuple-element.144.refs_3_), custom_call_target="tpu_custom_call" | custom-call | flops 3623878656 | bytes 8257536 | tf_op jit(solution)/shard_map/up_grad/pallas_call | solution.py:77
  96.7 12.6 %attend_back_0.1 = (bf16[768,384]{1,0:T(8,128)(2,1)}, bf16[768,384]{1,0:T(8,128)(2,1)}, bf16[768,384]{1,0:T(8,128)(2,1)}) custom-call(s32[28]{0:T(128)S(1)} %copy-done.13, f32[8,1280]{1,0:T(8,128)S(1)} %copy-done.10, f32[768]{0:T(1024)S(1)} %copy-done.6, bf16[768,768]{1,0:T(8,128)(2,1)} %get-tuple-element.126.refs_11_.refs_3_, ...), custom_call_target="tpu_custom_call" | custom-call | flops 8000000000 | bytes 5898240 | tf_op jit(solution)/shard_map/attend_back_0/pallas_call | solution.py:77
  109.3 4.6 %collective-permute-done.5 = bf16[384,768]{1,0:T(8,128)(2,1)S(1)} collective-permute-done((bf16[384,768]{1,0:T(8,128)(2,1)S(1)}, bf16[384,768]{1,0:T(8,128)(2,1)S(1)}, u32[]{:S(2)}, u32[]{:S(2)}) %collective-permute-start.5) | collective-permute-done | bytes 589856 | tf_op jit(solution)/shard_map/ppermute | solution.py:802
  118.1 7.0 %collective-permute-start.8 = (bf16[192,768]{1,0:T(8,128)(2,1)S(1)}, bf16[192,768]{1,0:T(8,128)(2,1)S(1)}, u32[]{:S(2)}, u32[]{:S(2)}) collective-permute-start(bf16[192,768]{1,0:T(8,128)(2,1)S(1)} %slice.318.refs_14_), channel_id=1, source_target_pairs={{0,4},{1,5},{2,6},{3,7},{4,0},{5,1},{6,2},{7,3},{8,12},{9,13},{10,... | collective-permute-start | bytes 884744 | tf_op jit(solution)/shard_map/ppermute | solution.py:802
  127.2 12.6 %attend_back_1.1 = (bf16[768,384]{1,0:T(8,128)(2,1)}, bf16[768,384]{1,0:T(8,128)(2,1)}, bf16[768,384]{1,0:T(8,128)(2,1)}) custom-call(s32[28]{0:T(128)S(1)} %copy-done.13, f32[8,1280]{1,0:T(8,128)S(1)} %copy-done.10, f32[768]{0:T(1024)S(1)} %copy-done.6, bf16[768,768]{1,0:T(8,128)(2,1)} %get-tuple-element.126.refs_11_.refs_3_, ...), custom_call_target="tpu_custom_call" | custom-call | flops 8000000000 | bytes 5898240 | tf_op jit(solution)/shard_map/attend_back_1/pallas_call | solution.py:77
  140.8 10.4 %rest_grad.1 = (bf16[1568,768]{1,0:T(8,128)(2,1)}, bf16[1568,768]{1,0:T(8,128)(2,1)}) custom-call(s32[3]{0:T(128)S(1)} %copy-done.1, f32[8,768]{1,0:T(8,128)S(1)} %copy-done.11, f32[8,768]{1,0:T(8,128)S(1)} %get-tuple-element.162.refs_2_, f32[4,768]{1,0:T(4,128)S(1)} %reshape.417.refs_3_, bf16[768,768]{1,0:T(8,128)(2,1)} %get-tuple-element.164.refs_4_, ...), custom_call_target="tpu_custom_call" | custom-call | flops 3623878656 | bytes 11796480 | tf_op jit(solution)/shard_map/rest_grad/pallas_call | solution.py:77
  155.1 3.9 %collective-permute-start.14 = (bf16[192,768]{1,0:T(8,128)(2,1)S(1)}, bf16[192,768]{1,0:T(8,128)(2,1)S(1)}, u32[]{:S(2)}, u32[]{:S(2)}) collective-permute-start(bf16[192,768]{1,0:T(8,128)(2,1)S(1)} %slice.329), channel_id=1, source_target_pairs={{0,4},{1,5},{2,6},{3,7},{4,0},{5,1},{6,2},{7,3},{8,12},{9,13},{10,... | collective-permute-start | bytes 884744 | tf_op jit(solution)/shard_map/ppermute | solution.py:802
  159.0 4.6 %collective-permute-start.18 = (bf16[96,768]{1,0:T(8,128)(2,1)S(1)}, bf16[96,768]{1,0:T(8,128)(2,1)S(1)}, u32[]{:S(2)}, u32[]{:S(2)}) collective-permute-start(bf16[96,768]{1,0:T(8,128)(2,1)S(1)} %bitcast.155), channel_id=1, source_target_pairs={{0,16},{8,24},{16,0},{24,8},{1,17},{9,25},{17,1},{25,9},{2,18},{10... | collective-permute-start | bytes 442376 | tf_op jit(solution)/shard_map/ppermute | solution.py:802
  163.6 8.4 %inputs_grad.1 = f32[768,768]{1,0:T(8,128)} custom-call(f32[768,768]{1,0:T(8,128)} %get-tuple-element.136.refs_0_, bf16[768,384]{1,0:T(8,128)(2,1)} %get-tuple-element.146.refs_7_.refs_1_, bf16[768,384]{1,0:T(8,128)(2,1)} %get-tuple-element.147.refs_8_.refs_2_, bf16[768,384]{1,0:T(8,128)(2,1)} %get-tuple-element.148.refs_9_.refs_3_, ...), custom_call_target="tpu_custom_call" | custom-call | flops 2717908992 | bytes 11796480 | tf_op jit(solution)/shard_map/inputs_grad/pallas_call | solution.py:77
  178.3 7.9 %collective-permute-done.20 = bf16[192,768]{1,0:T(8,128)(2,1)S(1)} collective-permute-done((bf16[192,768]{1,0:T(8,128)(2,1)S(1)}, bf16[192,768]{1,0:T(8,128)(2,1)S(1)}, u32[]{:S(2)}, u32[]{:S(2)}) %collective-permute-start.20) | collective-permute-done | bytes 294944 | tf_op jit(solution)/shard_map/ppermute | solution.py:802
  195.5 3.5 %collective-permute-done.23 = bf16[2,2,48,768]{3,2,0,1:T(8,128)(2,1)S(1)} collective-permute-done((bf16[2,2,48,768]{3,2,0,1:T(8,128)(2,1)S(1)}, bf16[2,2,48,768]{3,2,0,1:T(8,128)(2,1)S(1)}, u32[]{:S(2)}, u32[]{:S(2)}) %collective-permute-start.23) | collective-permute-done | bytes 294944 | tf_op jit(solution)/shard_map/ppermute | solution.py:802
  202.6 6.3 %collective-permute-done.22 = bf16[192,768]{1,0:T(8,128)(2,1)S(1)} collective-permute-done((bf16[192,768]{1,0:T(8,128)(2,1)S(1)}, bf16[192,768]{1,0:T(8,128)(2,1)S(1)}, u32[]{:S(2)}, u32[]{:S(2)}) %collective-permute-start.22) | collective-permute-done | bytes 294944 | tf_op jit(solution)/shard_map/ppermute | solution.py:802
  212.7 6.5 %collective-permute-done.25 = bf16[224,768]{1,0:T(8,128)(2,1)S(1)} collective-permute-done((bf16[224,768]{1,0:T(8,128)(2,1)S(1)}, bf16[224,768]{1,0:T(8,128)(2,1)S(1)}, u32[]{:S(2)}, u32[]{:S(2)}) %collective-permute-start.25) | collective-permute-done | bytes 344096 | tf_op jit(solution)/shard_map/ppermute | solution.py:802
  222.4 5.4 %collective-permute-done.29 = bf16[128,768]{1,0:T(8,128)(2,1)S(1)} collective-permute-done((bf16[128,768]{1,0:T(8,128)(2,1)S(1)}, bf16[128,768]{1,0:T(8,128)(2,1)S(1)}, u32[]{:S(2)}, u32[]{:S(2)}) %collective-permute-start.29) | collective-permute-done | bytes 196640 | tf_op jit(solution)/shard_map/ppermute | solution.py:802
  236.6 3.3 %collective-permute-done.32 = bf16[2,2,48,768]{3,2,1,0:T(8,128)(2,1)S(1)} collective-permute-done((bf16[2,2,48,768]{3,2,1,0:T(8,128)(2,1)S(1)}, bf16[2,2,48,768]{3,2,1,0:T(8,128)(2,1)S(1)}, u32[]{:S(2)}, u32[]{:S(2)}) %collective-permute-start.32) | collective-permute-done | bytes 294944 | tf_op jit(solution)/shard_map/ppermute | solution.py:802
  245.9 9.3 %spread_down.1 = f32[3072,768]{1,0:T(8,128)} custom-call(s32[3]{0:T(128)S(1)} %copy-done.1, bf16[8,192,768]{2,1,0:T(8,128)(2,1)} %bitcast.164, bf16[8,192,768]{2,1,0:T(8,128)(2,1)} %bitcast.165, bf16[8,192,768]{2,1,0:T(8,128)(2,1)} %copy-done.17, bf16[8,192,768]{2,1,0:T(8,128)(2,1)} %copy-done.17, bf16[2,2,48,768]{3,2,1,0:T(8,128)(2,1)S(1)} %copy.57.refs_5_), custom_call_target="tpu_custom_call" | custom-call | flops 2359296 | bytes 14155776 | tf_op jit(solution)/shard_map/spread_down/pallas_call | solution.py:77
  259.1 8.2 %collective-permute-done.38 = bf16[2,2,48,768]{3,2,1,0:T(8,128)(2,1)S(1)} collective-permute-done((bf16[2,2,48,768]{3,2,1,0:T(8,128)(2,1)S(1)}, bf16[2,2,48,768]{3,2,1,0:T(8,128)(2,1)S(1)}, u32[]{:S(2)}, u32[]{:S(2)}) %collective-permute-start.38) | collective-permute-done | bytes 294944 | tf_op jit(solution)/shard_map/ppermute | solution.py:802
  271.3 9.3 %spread_up.1 = f32[768,3072]{1,0:T(8,128)} custom-call(s32[3]{0:T(128)S(1)} %copy-done.1, bf16[8,192,768]{2,1,0:T(8,128)(2,1)} %bitcast.167, bf16[8,192,768]{2,1,0:T(8,128)(2,1)} %bitcast.168, bf16[8,192,768]{2,1,0:T(8,128)(2,1)} %copy-done.18, bf16[8,192,768]{2,1,0:T(8,128)(2,1)} %copy-done.18, bf16[2,2,2,48,768]{4,3,2,1,0:T(8,128)(2,1)S(1)} %get-tuple-element.221.refs_5_), custom_call_target="tpu_custom_call" | custom-call | flops 2359296 | bytes 14155776 | tf_op jit(solution)/shard_map/spread_up/pallas_call | solution.py:77
  284.8 3.2 %collective-permute-done.45.refs_3_.refs_4_ = bf16[8,192,768]{2,1,0:T(8,128)(2,1)} collective-permute-done((bf16[8,192,768]{2,1,0:T(8,128)(2,1)S(1)}, bf16[8,192,768]{2,1,0:T(8,128)(2,1)}, u32[]{:S(2)}, u32[]{:S(2)}) %collective-permute-start.45) | collective-permute-done | bytes 2359328 | tf_op jit(solution)/shard_map/ppermute | solution.py:802
  288.0 9.4 %spread_rest.1 = (f32[768,768]{1,0:T(8,128)}, f32[768,768]{1,0:T(8,128)}, f32[768,768]{1,0:T(8,128)}, f32[768,768]{1,0:T(8,128)}) custom-call(s32[3]{0:T(128)S(1)} %copy-done.1, bf16[8,192,768]{2,1,0:T(8,128)(2,1)} %bitcast.160, bf16[8,192,768]{2,1,0:T(8,128)(2,1)} %bitcast.161, bf16[8,192,768]{2,1,0:T(8,128)(2,1)} %collective-permute-done.45.refs_3_.refs_4_, ...), custom_call_target="tpu_custom_call" | custom-call | flops 2359296 | bytes 14155776 | tf_op jit(solution)/shard_map/spread_rest/pallas_call | solution.py:77
  (211 shorter events, 86.1 us)
Async XLA Ops:
  50.2 23.5 %collective-permute-start.4 = (bf16[1536,768]{1,0:T(8,128)(2,1)}, bf16[1536,768]{1,0:T(8,128)(2,1)S(1)}, u32[]{:S(2)}, u32[]{:S(2)}) collective-permute-start(bf16[1536,768]{1,0:T(8,128)(2,1)} %get-tuple-element.135.refs_9_), channel_id=1, source_target_pairs={{0,1},{1,0},{2,3},{3,2},{4,5},{5,4},{6,7},{7,6},{8,9},{9,8},{10,11... | collective-permute-start | bytes 7077896 | tf_op jit(solution)/shard_map/ppermute | solution.py:802
  84.7 29.7 %collective-permute-start.7 = (bf16[1536,768]{1,0:T(8,128)(2,1)}, bf16[1536,768]{1,0:T(8,128)(2,1)}, u32[]{:S(2)}, u32[]{:S(2)}) collective-permute-start(bf16[1536,768]{1,0:T(8,128)(2,1)} %get-tuple-element.145.refs_14_), channel_id=1, source_target_pairs={{0,1},{1,0},{2,3},{3,2},{4,5},{5,4},{6,7},{7,6},{8,9},{9,8},{10,11... | collective-permute-start | bytes 7077896 | tf_op jit(solution)/shard_map/ppermute | solution.py:802
  90.0 23.9 %collective-permute-start.5 = (bf16[384,768]{1,0:T(8,128)(2,1)S(1)}, bf16[384,768]{1,0:T(8,128)(2,1)S(1)}, u32[]{:S(2)}, u32[]{:S(2)}) collective-permute-start(bf16[384,768]{1,0:T(8,128)(2,1)S(1)} %get-tuple-element.144.refs_3_), channel_id=1, source_target_pairs={{0,2},{1,3},{2,0},{3,1},{4,6},{5,7},{6,4},{7,5},{8,10},{9,11},{10,... | collective-permute-start | bytes 1769480 | tf_op jit(solution)/shard_map/ppermute | solution.py:802
  93.1 20.9 %collective-permute-start.6 = (bf16[384,768]{1,0:T(8,128)(2,1)}, bf16[384,768]{1,0:T(8,128)(2,1)S(1)}, u32[]{:S(2)}, u32[]{:S(2)}) collective-permute-start(bf16[384,768]{1,0:T(8,128)(2,1)} %get-tuple-element.149), channel_id=1, source_target_pairs={{0,4},{1,5},{2,6},{3,7},{4,0},{5,1},{6,2},{7,3},{8,12},{9,13},{10,... | collective-permute-start | bytes 1769480 | tf_op jit(solution)/shard_map/ppermute | solution.py:802
  118.1 21.7 %collective-permute-start.8 = (bf16[192,768]{1,0:T(8,128)(2,1)S(1)}, bf16[192,768]{1,0:T(8,128)(2,1)S(1)}, u32[]{:S(2)}, u32[]{:S(2)}) collective-permute-start(bf16[192,768]{1,0:T(8,128)(2,1)S(1)} %slice.318.refs_14_), channel_id=1, source_target_pairs={{0,4},{1,5},{2,6},{3,7},{4,0},{5,1},{6,2},{7,3},{8,12},{9,13},{10,... | collective-permute-start | bytes 884744 | tf_op jit(solution)/shard_map/ppermute | solution.py:802
  125.1 14.8 %collective-permute-start.9 = (bf16[192,768]{1,0:T(8,128)(2,1)S(1)}, bf16[192,768]{1,0:T(8,128)(2,1)S(1)}, u32[]{:S(2)}, u32[]{:S(2)}) collective-permute-start(bf16[192,768]{1,0:T(8,128)(2,1)S(1)} %slice.320), channel_id=1, source_target_pairs={{0,2},{1,3},{2,0},{3,1},{4,6},{5,7},{6,4},{7,5},{8,10},{9,11},{10,... | collective-permute-start | bytes 884744 | tf_op jit(solution)/shard_map/ppermute | solution.py:802
  125.1 26.1 %collective-permute-start.11 = (bf16[384,768]{1,0:T(8,128)(2,1)S(1)}, bf16[384,768]{1,0:T(8,128)(2,1)S(1)}, u32[]{:S(2)}, u32[]{:S(2)}) collective-permute-start(bf16[384,768]{1,0:T(8,128)(2,1)S(1)} %get-tuple-element.168), channel_id=1, source_target_pairs={{0,2},{1,3},{2,0},{3,1},{4,6},{5,7},{6,4},{7,5},{8,10},{9,11},{10,... | collective-permute-start | bytes 1769480 | tf_op jit(solution)/shard_map/ppermute | solution.py:802
  127.1 24.1 %collective-permute-start.12 = (bf16[384,768]{1,0:T(8,128)(2,1)S(1)}, bf16[384,768]{1,0:T(8,128)(2,1)S(1)}, u32[]{:S(2)}, u32[]{:S(2)}) collective-permute-start(bf16[384,768]{1,0:T(8,128)(2,1)S(1)} %get-tuple-element.169), channel_id=1, source_target_pairs={{0,4},{1,5},{2,6},{3,7},{4,0},{5,1},{6,2},{7,3},{8,12},{9,13},{10,... | collective-permute-start | bytes 1769480 | tf_op jit(solution)/shard_map/ppermute | solution.py:802
  152.9 19.4 %collective-permute-start.13 = (bf16[1568,768]{1,0:T(8,128)(2,1)S(1)}, bf16[1568,768]{1,0:T(8,128)(2,1)S(1)}, u32[]{:S(2)}, u32[]{:S(2)}) collective-permute-start(bf16[1568,768]{1,0:T(8,128)(2,1)S(1)} %copy-done.23), channel_id=1, source_target_pairs={{0,1},{1,0},{2,3},{3,2},{4,5},{5,4},{6,7},{7,6},{8,9},{9,8},{10,11... | collective-permute-start | bytes 7225352 | tf_op jit(solution)/shard_map/ppermute | solution.py:802
  155.1 16.9 %collective-permute-start.14 = (bf16[192,768]{1,0:T(8,128)(2,1)S(1)}, bf16[192,768]{1,0:T(8,128)(2,1)S(1)}, u32[]{:S(2)}, u32[]{:S(2)}) collective-permute-start(bf16[192,768]{1,0:T(8,128)(2,1)S(1)} %slice.329), channel_id=1, source_target_pairs={{0,4},{1,5},{2,6},{3,7},{4,0},{5,1},{6,2},{7,3},{8,12},{9,13},{10,... | collective-permute-start | bytes 884744 | tf_op jit(solution)/shard_map/ppermute | solution.py:802
  159.0 13.0 %collective-permute-start.15 = (bf16[192,768]{1,0:T(8,128)(2,1)S(1)}, bf16[192,768]{1,0:T(8,128)(2,1)S(1)}, u32[]{:S(2)}, u32[]{:S(2)}) collective-permute-start(bf16[192,768]{1,0:T(8,128)(2,1)S(1)} %slice.331), channel_id=1, source_target_pairs={{0,2},{1,3},{2,0},{3,1},{4,6},{5,7},{6,4},{7,5},{8,10},{9,11},{10,... | collective-permute-start | bytes 884744 | tf_op jit(solution)/shard_map/ppermute | solution.py:802
  159.0 16.9 %collective-permute-start.18 = (bf16[96,768]{1,0:T(8,128)(2,1)S(1)}, bf16[96,768]{1,0:T(8,128)(2,1)S(1)}, u32[]{:S(2)}, u32[]{:S(2)}) collective-permute-start(bf16[96,768]{1,0:T(8,128)(2,1)S(1)} %bitcast.155), channel_id=1, source_target_pairs={{0,16},{8,24},{16,0},{24,8},{1,17},{9,25},{17,1},{25,9},{2,18},{10... | collective-permute-start | bytes 442376 | tf_op jit(solution)/shard_map/ppermute | solution.py:802
  175.9 15.5 %collective-permute-start.16 = (bf16[416,768]{1,0:T(8,128)(2,1)S(1)}, bf16[416,768]{1,0:T(8,128)(2,1)S(1)}, u32[]{:S(2)}, u32[]{:S(2)}) collective-permute-start(bf16[416,768]{1,0:T(8,128)(2,1)S(1)} %pad_maximum_fusion.3), channel_id=1, source_target_pairs={{0,2},{1,3},{2,0},{3,1},{4,6},{5,7},{6,4},{7,5},{8,10},{9,11},{10,... | collective-permute-start | bytes 1916936 | tf_op jit(solution)/shard_map/ppermute | solution.py:802
  176.5 14.1 %collective-permute-start.17 = (bf16[384,768]{1,0:T(8,128)(2,1)S(1)}, bf16[384,768]{1,0:T(8,128)(2,1)S(1)}, u32[]{:S(2)}, u32[]{:S(2)}) collective-permute-start(bf16[384,768]{1,0:T(8,128)(2,1)S(1)} %get-tuple-element.181), channel_id=1, source_target_pairs={{0,4},{1,5},{2,6},{3,7},{4,0},{5,1},{6,2},{7,3},{8,12},{9,13},{10,... | collective-permute-start | bytes 1769480 | tf_op jit(solution)/shard_map/ppermute | solution.py:802
  186.4 12.6 %collective-permute-start.23 = (bf16[2,2,48,768]{3,2,0,1:T(8,128)(2,1)S(1)}, bf16[2,2,48,768]{3,2,0,1:T(8,128)(2,1)S(1)}, u32[]{:S(2)}, u32[]{:S(2)}) collective-permute-start(bf16[2,2,48,768]{3,2,0,1:T(8,128)(2,1)S(1)} %get-tuple-element.290), channel_id=1, source_target_pairs={{0,8},{8,0},{16,24},{24,16},{1,9},{9,1},{17,25},{25,17},{2,10},{10... | collective-permute-start | bytes 884744 | tf_op jit(solution)/shard_map/ppermute | solution.py:802
  191.8 17.1 %collective-permute-start.21 = (bf16[224,768]{1,0:T(8,128)(2,1)S(1)}, bf16[224,768]{1,0:T(8,128)(2,1)S(1)}, u32[]{:S(2)}, u32[]{:S(2)}) collective-permute-start(bf16[224,768]{1,0:T(8,128)(2,1)S(1)} %pad_maximum_fusion.10), channel_id=1, source_target_pairs={{0,4},{1,5},{2,6},{3,7},{4,0},{5,1},{6,2},{7,3},{8,12},{9,13},{10,... | collective-permute-start | bytes 1032200 | tf_op jit(solution)/shard_map/ppermute | solution.py:802
  193.8 15.5 %collective-permute-start.28 = (bf16[2,48,768]{2,1,0:T(8,128)(2,1)S(1)}, bf16[2,48,768]{2,1,0:T(8,128)(2,1)S(1)}, u32[]{:S(2)}, u32[]{:S(2)}) collective-permute-start(bf16[2,48,768]{2,1,0:T(8,128)(2,1)S(1)} %fusion.10), channel_id=1, source_target_pairs={{0,16},{8,24},{16,0},{24,8},{1,17},{9,25},{17,1},{25,9},{2,18},{10... | collective-permute-start | bytes 442376 | tf_op jit(solution)/shard_map/ppermute | solution.py:802
  199.1 12.4 %collective-permute-start.26 = (bf16[2,2,48,768]{3,2,1,0:T(8,128)(2,1)S(1)}, bf16[2,2,48,768]{3,2,1,0:T(8,128)(2,1)S(1)}, u32[]{:S(2)}, u32[]{:S(2)}) collective-permute-start(bf16[2,2,48,768]{3,2,1,0:T(8,128)(2,1)S(1)} %get-tuple-element.192), channel_id=1, source_target_pairs={{0,4},{1,5},{2,6},{3,7},{4,0},{5,1},{6,2},{7,3},{8,12},{9,13},{10,... | collective-permute-start | bytes 884744 | tf_op jit(solution)/shard_map/ppermute | solution.py:802
  209.4 13.0 %collective-permute-start.30 = (bf16[2,2,48,768]{3,2,0,1:T(8,128)(2,1)S(1)}, bf16[2,2,48,768]{3,2,0,1:T(8,128)(2,1)S(1)}, u32[]{:S(2)}, u32[]{:S(2)}) collective-permute-start(bf16[2,2,48,768]{3,2,0,1:T(8,128)(2,1)S(1)} %get-tuple-element.288), channel_id=1, source_target_pairs={{0,8},{8,0},{16,24},{24,16},{1,9},{9,1},{17,25},{25,17},{2,10},{10... | collective-permute-start | bytes 884744 | tf_op jit(solution)/shard_map/ppermute | solution.py:802
  230.4 14.0 %collective-permute-start.37 = (bf16[8,192,768]{2,1,0:T(8,128)(2,1)S(1)}, bf16[8,192,768]{2,1,0:T(8,128)(2,1)S(1)}, u32[]{:S(2)}, u32[]{:S(2)}) collective-permute-start(bf16[8,192,768]{2,1,0:T(8,128)(2,1)S(1)} %bitcast.163), channel_id=1, source_target_pairs={{0,1},{1,0},{2,3},{3,2},{4,5},{5,4},{6,7},{7,6},{8,9},{9,8},{10,11... | collective-permute-start | bytes 7077896 | tf_op jit(solution)/shard_map/ppermute | solution.py:802
  241.5 14.6 %collective-permute-start.40 = (bf16[2,2,2,48,768]{4,3,2,1,0:T(8,128)(2,1)S(1)}, bf16[2,2,2,48,768]{4,3,2,1,0:T(8,128)(2,1)S(1)}, u32[]{:S(2)}, u32[]{:S(2)}) collective-permute-start(bf16[2,2,2,48,768]{4,3,2,1,0:T(8,128)(2,1)S(1)} %get-tuple-element.210), channel_id=1, source_target_pairs={{0,2},{1,3},{2,0},{3,1},{4,6},{5,7},{6,4},{7,5},{8,10},{9,11},{10,... | collective-permute-start | bytes 1769480 | tf_op jit(solution)/shard_map/ppermute | solution.py:802
  243.1 14.3 %collective-permute-start.41 = (bf16[2,2,2,48,768]{4,3,2,1,0:T(8,128)(2,1)S(1)}, bf16[2,2,2,48,768]{4,3,2,1,0:T(8,128)(2,1)S(1)}, u32[]{:S(2)}, u32[]{:S(2)}) collective-permute-start(bf16[2,2,2,48,768]{4,3,2,1,0:T(8,128)(2,1)S(1)} %get-tuple-element.216), channel_id=1, source_target_pairs={{0,4},{1,5},{2,6},{3,7},{4,0},{5,1},{6,2},{7,3},{8,12},{9,13},{10,... | collective-permute-start | bytes 1769480 | tf_op jit(solution)/shard_map/ppermute | solution.py:802
  267.8 14.6 %collective-permute-start.42 = (bf16[2,2,2,48,768]{4,3,2,1,0:T(8,128)(2,1)S(1)}, bf16[2,2,2,48,768]{4,3,2,1,0:T(8,128)(2,1)S(1)}, u32[]{:S(2)}, u32[]{:S(2)}) collective-permute-start(bf16[2,2,2,48,768]{4,3,2,1,0:T(8,128)(2,1)S(1)} %get-tuple-element.221.refs_5_), channel_id=1, source_target_pairs={{0,2},{1,3},{2,0},{3,1},{4,6},{5,7},{6,4},{7,5},{8,10},{9,11},{10,... | collective-permute-start | bytes 1769480 | tf_op jit(solution)/shard_map/ppermute | solution.py:802
  268.5 14.3 %collective-permute-start.43 = (bf16[2,2,2,48,768]{4,3,2,1,0:T(8,128)(2,1)S(1)}, bf16[2,2,2,48,768]{4,3,2,1,0:T(8,128)(2,1)S(1)}, u32[]{:S(2)}, u32[]{:S(2)}) collective-permute-start(bf16[2,2,2,48,768]{4,3,2,1,0:T(8,128)(2,1)S(1)} %get-tuple-element.222), channel_id=1, source_target_pairs={{0,4},{1,5},{2,6},{3,7},{4,0},{5,1},{6,2},{7,3},{8,12},{9,13},{10,... | collective-permute-start | bytes 1769480 | tf_op jit(solution)/shard_map/ppermute | solution.py:802
  (48 other events, 364.5 us)
